TPU v7x, 128 devices: a whole 4x4x4 slice. The times are simulated.
128 devices in a mesh: dp: 4 (over z), expert: 32 (over x, y, core).
Axes of the slice: x: 4, y: 4, z: 4, core: 2. Of those that a mesh axis runs over, the one named last changes fastest.
Arguments:
- tokens: bfloat16 [32768, 768], P(('dp', 'expert')), may hold values from -6 to 6
- segment_ids: int32 [128, 256], P(('dp', 'expert')), may hold values from 0 to 3, never falling along the last dimension, each value on 1 to 128 neighbouring positions
- routes: int32 [32768, 2], P(('dp', 'expert')), may hold values from 0 to 32, all different within a row; in each aligned block of 256 rows (0 to 255, 256 to 511, ...) at most 24 rows name the same one
- cotangent: bfloat16 [32768, 768], P(('dp', 'expert')), may hold values from -6 to 6
- w_qkv: bfloat16 [768, 2304], replicated, may hold values from -0.21875 to 0.21875
- w_attn_out: bfloat16 [768, 768], replicated, may hold values from -0.875 to 0.875
- w_router: bfloat16 [768, 33], replicated, may hold values from -0.15625 to 0.15625
- norm_gains: float32 [2, 768], replicated, may hold values from 0.5 to 1.5
- frozen_in: bfloat16 [768, 3072], replicated, may hold values from -0.21875 to 0.21875
- frozen_out: bfloat16 [3072, 768], replicated, may hold values from -0.109375 to 0.109375
- new_in: bfloat16 [32, 768, 3072], P('expert', 'dp'), may hold values from -0.21875 to 0.21875
- new_out: bfloat16 [32, 3072, 768], P('expert', 'dp'), may hold values from -0.109375 to 0.109375
- dense_master: float32 [2392064], P(('dp', 'expert'))
- dense_first: float32 [2392064], P(('dp', 'expert'))
- dense_second: float32 [2392064], P(('dp', 'expert')), as said below
- master_in: float32 [32, 768, 3072], P('expert', 'dp'), may hold values from -0.4375 to 0.4375
- first_in: float32 [32, 768, 3072], P('expert', 'dp'), may hold values from -32 to 32
- second_in: float32 [32, 768, 3072], P('expert', 'dp'), may hold values from 28.597527 to 114.39011
- master_out: float32 [32, 3072, 768], P('expert', 'dp'), may hold values from -0.4375 to 0.4375
- first_out: float32 [32, 3072, 768], P('expert', 'dp'), may hold values from -80 to 80
- second_out: float32 [32, 3072, 768], P('expert', 'dp'), may hold values from 178.73454 to 714.9382
Outputs:
- activations: bfloat16 [32768, 768], P(('dp', 'expert'))
- input_grad: float32 [32768, 768], P(('dp', 'expert'))
- dense_master_new: float32 [2392064], P(('dp', 'expert'))
- dense_first_new: float32 [2392064], P(('dp', 'expert'))
- dense_second_new: float32 [2392064], P(('dp', 'expert'))
- dense_copy: bfloat16 [2392064], P(('dp', 'expert'))
- in_master_new: float32 [32, 768, 3072], P('expert', 'dp')
- in_first_new: float32 [32, 768, 3072], P('expert', 'dp')
- in_second_new: float32 [32, 768, 3072], P('expert', 'dp')
- in_copy: bfloat16 [32, 768, 3072], P('expert', 'dp')
- out_master_new: float32 [32, 3072, 768], P('expert', 'dp')
- out_first_new: float32 [32, 3072, 768], P('expert', 'dp')
- out_second_new: float32 [32, 3072, 768], P('expert', 'dp')
- out_copy: bfloat16 [32, 3072, 768], P('expert', 'dp')
Inputs may be any that keep to these rules, and one draw needn't show every extreme that they name: `routes`: in the 256 rows of one device no expert is named by more than 24 rows, and in every draw some expert is named by exactly 24 rows of some device; a row names two different experts. `segment_ids`: ids never fall along a row; an id covers 1 to 128 positions, some id exactly that many. `dense_second`: every entry is positive.
All inputs are finite; a program needn't handle non-finite values.
Results may differ from a plain program's by a relative error of at most 0.018.
Values may be sent and summed in bfloat16 or wider, within the bound.
No kernel may reach another device: no remote copies, remote signals or barrier semaphores. Data moves between devices by JAX's collectives and lax.ppermute only.
A program may use at most 192 MiB of HBM per device.

v0:
```python
import jax
import jax.numpy as jnp
from jax import lax
from jax.sharding import PartitionSpec as P

HEAD_DIM = 64
STEP = 5


norm_eps = 1e-05
learn_rate = 0.02
beta_first = 0.5
beta_second = 0.5
adam_eps = 1e-08
decay_rate = 0.1


def layer_norm(values, gain_row):
    centered = values - jnp.mean(values, axis=-1, keepdims=True)
    variance = jnp.mean(centered * centered, axis=-1, keepdims=True)
    return centered * lax.rsqrt(variance + norm_eps) * gain_row


def norm_back(values, gain_row, upstream):
    unused, pullback = jax.vjp(layer_norm, values, gain_row)
    return pullback(upstream)


def exact_gelu(pre_act):
    return jax.nn.gelu(pre_act, approximate=False)


def split_heads(qkv_low):
    seq_length = qkv_low.shape[0]
    model_width = qkv_low.shape[1] // 3
    head_count = model_width // HEAD_DIM
    queries = qkv_low[:, :model_width].reshape(seq_length, head_count, HEAD_DIM)
    key_rows = qkv_low[:, model_width : 2 * model_width].reshape(seq_length, head_count, HEAD_DIM)
    value_rows = qkv_low[:, 2 * model_width :].reshape(seq_length, head_count, HEAD_DIM)
    return (queries, key_rows, value_rows)


def masked_scores(queries, key_rows, segment_row):
    positions = jnp.arange(segment_row.shape[0])
    allowed = (positions[:, None] >= positions[None, :]) & (
        segment_row[:, None] == segment_row[None, :]
    )
    scores = jnp.einsum(
        "thd,shd->hts", queries, key_rows, preferred_element_type=jnp.float32
    ) * HEAD_DIM ** (-0.5)
    return jnp.where(allowed[None], scores, -1e30)


def attention_forward(qkv_low, segment_row):
    queries, key_rows, value_rows = split_heads(qkv_low)
    scores = masked_scores(queries, key_rows, segment_row)
    log_totals = jax.nn.logsumexp(scores, axis=-1, keepdims=True)
    probs_low = jnp.exp(scores - log_totals).astype(jnp.bfloat16)
    mixed_out = jnp.einsum(
        "hts,shd->thd", probs_low, value_rows, preferred_element_type=jnp.float32
    )
    return (mixed_out.reshape(qkv_low.shape[0], -1).astype(jnp.bfloat16), log_totals)


def attention_backward(qkv_low, segment_row, log_totals, grad_mixed):
    queries, key_rows, value_rows = split_heads(qkv_low)
    scores = masked_scores(queries, key_rows, segment_row)
    probs_full = jnp.exp(scores - log_totals)
    grad_heads = grad_mixed.reshape(queries.shape)
    grad_probs = jnp.einsum(
        "thd,shd->hts", grad_heads, value_rows, preferred_element_type=jnp.float32
    )
    grad_values = jnp.einsum(
        "hts,thd->shd",
        probs_full.astype(jnp.bfloat16),
        grad_heads,
        preferred_element_type=jnp.float32,
    )
    row_dots = jnp.sum(probs_full * grad_probs, axis=-1, keepdims=True)
    grad_scores = (probs_full * (grad_probs - row_dots)).astype(jnp.bfloat16)
    grad_queries = jnp.einsum(
        "hts,shd->thd", grad_scores, key_rows, preferred_element_type=jnp.float32
    ) * HEAD_DIM ** (-0.5)
    grad_keys = jnp.einsum(
        "hts,thd->shd", grad_scores, queries, preferred_element_type=jnp.float32
    ) * HEAD_DIM ** (-0.5)
    seq_length = qkv_low.shape[0]
    return jnp.concatenate(
        [
            grad_queries.reshape(seq_length, -1),
            grad_keys.reshape(seq_length, -1),
            grad_values.reshape(seq_length, -1),
        ],
        axis=1,
    )


def expert_forward(row_block, weight_in, weight_out):
    pre_act = jnp.dot(row_block, weight_in, preferred_element_type=jnp.float32)
    hidden = exact_gelu(pre_act).astype(jnp.bfloat16)
    result = jnp.dot(hidden, weight_out, preferred_element_type=jnp.float32).astype(jnp.bfloat16)
    return (pre_act, result)


def expert_backward(pre_act, grad_result, weight_in, weight_out):
    grad_hidden = jnp.einsum(
        "rd,fd->rf", grad_result, weight_out, preferred_element_type=jnp.float32
    )
    hidden, gelu_pull = jax.vjp(exact_gelu, pre_act)
    grad_pre = gelu_pull(grad_hidden)[0].astype(jnp.bfloat16)
    grad_rows = jnp.einsum(
        "rf,df->rd", grad_pre, weight_in, preferred_element_type=jnp.float32
    ).astype(jnp.bfloat16)
    return (hidden.astype(jnp.bfloat16), grad_pre, grad_rows)


def adamw(master, first, second, grad):
    first_new = beta_first * first + (1.0 - beta_first) * grad
    second_new = beta_second * second + (1.0 - beta_second) * grad * grad
    first_hat = first_new / (1.0 - beta_first**STEP)
    second_hat = second_new / (1.0 - beta_second**STEP)
    master_new = master - learn_rate * (
        first_hat / (jnp.sqrt(second_hat) + adam_eps) + decay_rate * master
    )
    return (master_new, first_new, second_new, master_new.astype(jnp.bfloat16))


def body(
    tokens,
    segment_ids,
    routes,
    cotangent,
    w_qkv,
    w_attn_out,
    w_router,
    norm_gains,
    frozen_in,
    frozen_out,
    new_in,
    new_out,
    dense_master,
    dense_first,
    dense_second,
    master_in,
    first_in,
    second_in,
    master_out,
    first_out,
    second_out,
):
    token_count, model_width = tokens.shape
    hidden_width = frozen_in.shape[1]
    expert_total = w_router.shape[1]
    capacity = 3 * token_count // expert_total + 1
    source_count = lax.axis_size("expert")
    group_count = lax.axis_size("dp")
    full_in, full_out = (
        lax.all_gather(new_in, "dp", axis=1, tiled=True),
        lax.all_gather(new_out, "dp", axis=1, tiled=True),
    )
    full_in = full_in[0]
    full_out = full_out[0]
    inputs = tokens.astype(jnp.float32)
    attn_in = layer_norm(inputs, norm_gains[0]).astype(jnp.bfloat16)
    qkv_low = jnp.dot(attn_in, w_qkv, preferred_element_type=jnp.float32).astype(jnp.bfloat16)
    mixed_low, log_totals = attention_forward(qkv_low, segment_ids[0])
    middle = inputs + jnp.dot(mixed_low, w_attn_out, preferred_element_type=jnp.float32)
    feedforward_input = layer_norm(middle, norm_gains[1]).astype(jnp.bfloat16)
    logits = jnp.dot(feedforward_input, w_router, preferred_element_type=jnp.float32)
    expert_ids = jnp.arange(expert_total, dtype=jnp.int32)
    picked = (routes[:, :, None] == expert_ids[None, None, :]).astype(jnp.float32)
    chosen = jnp.sum(picked * logits[:, None, :], axis=-1)
    gate_values = jax.nn.softmax(chosen, axis=-1)
    flat_routes = routes.reshape(-1)
    onehot = (flat_routes[:, None] == expert_ids[None, :]).astype(jnp.int32)
    before = jnp.cumsum(onehot, axis=0) - onehot
    places = flat_routes * capacity + jnp.sum(before * onehot, axis=1)
    select_rows = (
        places[:, None] == jnp.arange(expert_total * capacity, dtype=jnp.int32)[None, :]
    ).astype(jnp.bfloat16)
    select_rows = select_rows.reshape(token_count, 2, expert_total * capacity)
    state_buffers = jnp.einsum(
        "lkp,ld->pd", select_rows, feedforward_input, preferred_element_type=jnp.float32
    ).astype(jnp.bfloat16)
    state_buffers = state_buffers.reshape(expert_total, capacity, model_width)
    frozen_pre, frozen_result = expert_forward(state_buffers[0], frozen_in, frozen_out)
    upstream = cotangent.astype(jnp.float32)
    grad_pairs = (gate_values[:, :, None] * upstream[:, None, :]).astype(jnp.bfloat16)
    grad_results = jnp.einsum(
        "lkp,lkd->pd", select_rows, grad_pairs, preferred_element_type=jnp.float32
    ).astype(jnp.bfloat16)
    grad_results = grad_results.reshape(expert_total, capacity, model_width)
    received = lax.all_to_all(state_buffers[1:], "expert", split_axis=0, concat_axis=0, tiled=True)
    pre_act, result = expert_forward(received.reshape(-1, model_width), full_in, full_out)
    sent_back = lax.all_to_all(
        result.reshape(received.shape), "expert", split_axis=0, concat_axis=0, tiled=True
    )
    sent_back, pre_act = (sent_back, pre_act)
    new_pre = pre_act.reshape(received.shape[0], received.shape[1], -1)
    new_pre = new_pre.reshape(-1, hidden_width)
    grad_received = lax.all_to_all(
        grad_results[1:], "expert", split_axis=0, concat_axis=0, tiled=True
    )
    grad_out_rows = grad_received.reshape(-1, model_width)
    new_hidden, new_grad_pre, new_grad_rows = expert_backward(
        new_pre, grad_out_rows, full_in, full_out
    )
    grad_back = lax.all_to_all(
        new_grad_rows.reshape(source_count, capacity, model_width),
        "expert",
        split_axis=0,
        concat_axis=0,
        tiled=True,
    )
    results = jnp.concatenate([frozen_result[None], sent_back], axis=0).reshape(
        expert_total * capacity, model_width
    )
    pair_values = jnp.einsum(
        "lkp,pd->lkd", select_rows, results, preferred_element_type=jnp.float32
    )
    activations = middle + jnp.sum(gate_values[:, :, None] * pair_values, axis=1)
    grad_gates = jnp.sum(upstream[:, None, :] * pair_values, axis=-1)
    grad_chosen = gate_values * (
        grad_gates - jnp.sum(gate_values * grad_gates, axis=-1, keepdims=True)
    )
    grad_logits = jnp.sum(picked * grad_chosen[:, :, None], axis=1).astype(jnp.bfloat16)
    router_grad = jnp.einsum(
        "ld,le->de", feedforward_input, grad_logits, preferred_element_type=jnp.float32
    )
    grad_ffn = jnp.einsum("le,de->ld", grad_logits, w_router, preferred_element_type=jnp.float32)
    frozen_parts = expert_backward(frozen_pre, grad_results[0], frozen_in, frozen_out)
    in_rows = received.reshape(-1, model_width)
    grad_in_full = jnp.einsum(
        "rd,rf->df", in_rows, new_grad_pre, preferred_element_type=jnp.float32
    )
    grad_out_full = jnp.einsum(
        "rf,rd->fd", new_hidden, grad_out_rows, preferred_element_type=jnp.float32
    )
    grad_in_shard, grad_out_shard = (
        lax.psum_scatter(
            grad_in_full.astype(jnp.bfloat16), "dp", scatter_dimension=0, tiled=True
        ).astype(jnp.float32),
        lax.psum_scatter(
            grad_out_full.astype(jnp.bfloat16), "dp", scatter_dimension=0, tiled=True
        ).astype(jnp.float32),
    )
    grad_buffers = jnp.concatenate([frozen_parts[2][None], grad_back], axis=0).reshape(
        -1, model_width
    )
    grad_ffn = grad_ffn + jnp.einsum(
        "lkp,pd->ld", select_rows, grad_buffers, preferred_element_type=jnp.float32
    )
    grad_middle_norm, gain_ffn_grad = norm_back(middle, norm_gains[1], grad_ffn)
    grad_middle = upstream + grad_middle_norm
    grad_branch = grad_middle.astype(jnp.bfloat16)
    attn_out_grad = jnp.einsum(
        "ld,le->de", mixed_low, grad_branch, preferred_element_type=jnp.float32
    )
    grad_mixed = jnp.einsum(
        "le,de->ld", grad_branch, w_attn_out, preferred_element_type=jnp.float32
    ).astype(jnp.bfloat16)
    grad_qkv = attention_backward(qkv_low, segment_ids[0], log_totals, grad_mixed).astype(
        jnp.bfloat16
    )
    qkv_grad = jnp.einsum("ld,le->de", attn_in, grad_qkv, preferred_element_type=jnp.float32)
    grad_attn_norm = jnp.einsum("le,de->ld", grad_qkv, w_qkv, preferred_element_type=jnp.float32)
    grad_input_norm, gain_attn_grad = norm_back(inputs, norm_gains[0], grad_attn_norm)
    input_grad = grad_middle + grad_input_norm
    device_total = group_count * source_count
    flat_grad = jnp.concatenate(
        [
            qkv_grad.reshape(-1),
            attn_out_grad.reshape(-1),
            router_grad.reshape(-1),
            gain_attn_grad,
            gain_ffn_grad,
        ]
    )
    flat_grad = jnp.concatenate(
        [
            flat_grad,
            jnp.zeros((dense_master.shape[0] * device_total - flat_grad.shape[0],), jnp.float32),
        ]
    )
    dense_grad = lax.psum_scatter(flat_grad, ("dp", "expert"), scatter_dimension=0, tiled=True)
    dense_new = adamw(dense_master, dense_first, dense_second, dense_grad)
    in_new = adamw(master_in, first_in, second_in, grad_in_shard[None])
    out_new = adamw(master_out, first_out, second_out, grad_out_shard[None])
    return (
        activations.astype(jnp.bfloat16),
        input_grad,
        dense_new[0],
        dense_new[1],
        dense_new[2],
        dense_new[3],
        in_new[0],
        in_new[1],
        in_new[2],
        in_new[3],
        out_new[0],
        out_new[1],
        out_new[2],
        out_new[3],
    )


def solution(mesh):
    return jax.shard_map(
        body,
        mesh=mesh,
        in_specs=(
            P(("dp", "expert"), None),
            P(("dp", "expert"), None),
            P(("dp", "expert"), None),
            P(("dp", "expert"), None),
            P(),
            P(),
            P(),
            P(),
            P(),
            P(),
            P("expert", "dp", None),
            P("expert", "dp", None),
            P(("dp", "expert")),
            P(("dp", "expert")),
            P(("dp", "expert")),
            P("expert", "dp", None),
            P("expert", "dp", None),
            P("expert", "dp", None),
            P("expert", "dp", None),
            P("expert", "dp", None),
            P("expert", "dp", None),
        ),
        out_specs=(
            P(("dp", "expert"), None),
            P(("dp", "expert"), None),
            P(("dp", "expert")),
            P(("dp", "expert")),
            P(("dp", "expert")),
            P(("dp", "expert")),
            P("expert", "dp", None),
            P("expert", "dp", None),
            P("expert", "dp", None),
            P("expert", "dp", None),
            P("expert", "dp", None),
            P("expert", "dp", None),
            P("expert", "dp", None),
            P("expert", "dp", None),
        ),
        check_vma=False,
    )
```

profile of v0, /device:TPU:0, one launch (start us, length us, event | category | flops | bytes accessed | tf_op | source)
XLA Modules:
  0.0 515.9 jit_solution(11210835783866294997)
XLA Ops:
  7.9 1.8 copy.108
  9.7 1.0 eq.111
  10.8 1.0 eq.107
  12.5 3.2 reduce-window.6
  15.7 1.1 slice_reduce_fusion
  20.5 1.2 convert_reduce_fusion.1
  21.7 1.3 fusion.48
  23.6 2.2 convolution_convert_fusion.2
  25.8 1.0 fusion.115
  26.8 1.9 copy.106
  28.7 1.9 copy.105
  30.7 1.9 copy.104
  33.8 1.9 fusion.16
  42.6 1.1 slice.64
  43.6 7.5 %all-to-all-start = ((bf16[32,24,768]{2,1,0:T(8,128)(2,1)}), bf16[32,24,768]{2,1,0:T(8,128)(2,1)}, u32[]{:S(2)}, u32[]{:S(2)}) async-start(bf16[32,24,768]{2,1,0:T(8,128)(2,1)} %bitcast.125), calls=%async_computation | async-start | bytes 2359296 | tf_op jit(solution)/shard_map/all_to_all | solution.py:193
  51.9 1.9 convert_element_type.133
  53.9 1.2 fusion.117
  55.3 2.1 bitcast_convert_fusion
  57.4 1.2 slice.66
  58.6 3.1 fusion.78
  62.4 4.2 fusion.40
  66.5 7.2 %fusion.41 = bf16[1,24,768]{2,1,0:T(8,128)(2,1)} fusion(bf16[768,3072]{1,0:T(8,128)(2,1)} %param.29, f32[24,3072]{1,0:T(8,128)} %copy-done.30, bf16[3072,768]{1,0:T(8,128)(2,1)} %param.30, bf16[792,768]{1,0:T(8,128)(2,1)} %copy-done.27), kind=kOutput, calls=%fused_computation.83 | convolution fusion | flops 231819264 | bytes 9805824 | tf_op jit(solution)/shard_map/rf,df->rd/dot_general | solution.py:111
  73.7 8.0 %all-to-all-start.2 = ((bf16[32,24,768]{2,1,0:T(8,128)(2,1)}), bf16[32,24,768]{2,1,0:T(8,128)(2,1)}, u32[]{:S(2)}, u32[]{:S(2)}) async-start(bf16[32,24,768]{2,1,0:T(8,128)(2,1)} %bitcast.126), calls=%async_computation.2 | async-start | bytes 2359296 | tf_op jit(solution)/shard_map/all_to_all | solution.py:201
  81.7 26.9 %multiply_convert_fusion = (bf16[768,3072]{1,0:T(8,128)(2,1)}, f32[768,3072]{1,0:T(8,128)}, f32[768,3072]{1,0:T(8,128)}) fusion(bf16[768,768]{1,0:T(8,128)(2,1)} %bitcast.10, bf16[1,768,3072]{2,1,0:T(8,128)(2,1)} %all-gather.3.cloned.1.call-done), kind=kOutput, calls=%fused_computation.3 | convolution fusion | flops 3777232896 | bytes 29491200 | tf_op jit(solution)/shard_map/dot_general | solution.py:99
  108.6 11.2 %all-gather.5.cloned.1.call-done = bf16[1,3072,768]{2,1,0:T(8,128)(2,1)} async-done(((bf16[1,768,768]{2,1,0:T(8,128)(2,1)}), bf16[1,3072,768]{2,1,0:T(8,128)(2,1)}) %all-gather.5.cloned.1.call-update) | async-done | bytes 4718608 | tf_op jit(solution)/shard_map/all_gather | solution.py:159
  119.8 8.6 %fusion.31 = bf16[768,768]{1,0:T(8,128)(2,1)} fusion(bf16[768,3072]{1,0:T(8,128)(2,1)} %get-tuple-element.36, bf16[1,3072,768]{2,1,0:T(8,128)(2,1)} %all-gather.5.cloned.1.call-done), kind=kOutput, calls=%fused_computation.59 | convolution fusion | flops 3624468480 | bytes 10616832 | tf_op jit(solution)/shard_map/dot_general | solution.py:101
  128.4 7.4 %all-to-all-start.1 = ((bf16[32,24,768]{2,1,0:T(8,128)(2,1)}), bf16[32,24,768]{2,1,0:T(8,128)(2,1)}, u32[]{:S(2)}, u32[]{:S(2)}) async-start(bf16[32,24,768]{2,1,0:T(8,128)(2,1)} %bitcast.143), calls=%async_computation.1 | async-start | bytes 2359296 | tf_op jit(solution)/shard_map/all_to_all | solution.py:195
  135.8 12.4 %add_convert_fusion = bf16[768,3072]{1,0:T(8,128)(2,1)S(1)} fusion(f32[768,3072]{1,0:T(8,128)} %get-tuple-element.37, f32[768,3072]{1,0:T(8,128)} %get-tuple-element.46, bf16[768,768]{1,0:T(8,128)(2,1)} %bitcast.19, bf16[1,3072,768]{2,1,0:T(8,128)(2,1)} %all-gather.5.cloned.1.call-done), kind=kOutput, calls=%fused_computation.2 | convolution fusion | flops 3656908800 | bytes 29491200 | tf_op jit(solution)/shard_map/rd,fd->rf/dot_general | solution.py:106
  148.2 2.2 copy-done.59
  150.4 7.2 %fusion.28 = bf16[768,768]{1,0:T(8,128)(2,1)} fusion(bf16[768,3072]{1,0:T(8,128)(2,1)S(1)} %add_convert_fusion, bf16[1,768,3072]{2,1,0:T(8,128)(2,1)} %all-gather.3.cloned.1.call-done), kind=kOutput, calls=%fused_computation.58 | convolution fusion | flops 3624468480 | bytes 10616832 | tf_op jit(solution)/shard_map/rf,df->rd/dot_general | solution.py:111
  157.7 7.6 %all-to-all-start.3 = ((bf16[32,24,768]{2,1,0:T(8,128)(2,1)}), bf16[32,24,768]{2,1,0:T(8,128)(2,1)}, u32[]{:S(2)}, u32[]{:S(2)}) async-start(bf16[32,24,768]{2,1,0:T(8,128)(2,1)} %bitcast.142), calls=%async_computation.3 | async-start | bytes 2359296 | tf_op jit(solution)/shard_map/all_to_all | solution.py:208
  165.6 1.4 pad_maximum_fusion
  167.0 3.4 multiply_reduce_fusion.1
  170.6 1.1 fusion.119
  171.6 1.2 fusion.120
  172.8 10.9 %all-to-all-done.3 = bf16[32,24,768]{2,1,0:T(8,128)(2,1)} async-done(((bf16[32,24,768]{2,1,0:T(8,128)(2,1)}), bf16[32,24,768]{2,1,0:T(8,128)(2,1)}, u32[]{:S(2)}, u32[]{:S(2)}) %all-to-all-start.3) | async-done | bytes 1179680 | tf_op jit(solution)/shard_map/all_to_all | solution.py:208
  183.7 1.5 pad_maximum_fusion.1
  185.2 3.0 multiply_reduce_fusion.3
  188.3 1.1 fusion.113
  189.4 1.3 convolution_convert_fusion.5
  190.7 2.0 fusion.61
  192.7 1.9 copy.112
  194.6 2.9 convolution_convert_fusion.4
  197.7 1.1 multiply_reduce_fusion
  200.8 2.6 fusion.49
  203.5 4.2 fusion.52
  207.7 1.9 reshape.370
  209.6 3.2 reshape.369
  213.5 7.9 %reshape.368 = f32[1769472]{0:T(1024)} reshape(f32[768,2304]{1,0:T(8,128)} %fusion.52) | data formatting | bytes 14155776 | tf_op jit(solution)/shard_map/reshape | solution.py:272
  221.4 5.6 %constant_dynamic-update-slice_fusion.4 = f32[2392064]{0:T(1024)} fusion(f32[1769472]{0:T(1024)} %reshape.368), kind=kLoop, calls=%fused_computation.159 | loop fusion | bytes 14155776
  228.1 1.5 constant_dynamic-update-slice_fusion.3
  229.6 1.5 constant_dynamic-update-slice_fusion.2
  231.2 1.3 constant_dynamic-update-slice_fusion.1
  232.5 1.3 constant_dynamic-update-slice_fusion
  233.8 1.3 broadcast_dynamic-update-slice_fusion
  235.4 8.7 %convolution_convert_fusion.1 = bf16[768,3072]{1,0:T(8,128)(2,1)} fusion(bf16[768,768]{1,0:T(8,128)(2,1)} %bitcast.10, bf16[768,3072]{1,0:T(8,128)(2,1)} %copy-done.59), kind=kOutput, calls=%fused_computation.18 | convolution fusion | flops 3626237952 | bytes 10616832 | tf_op jit(solution)/shard_map/rd,rf->df/dot_general | solution.py:233
  244.2 9.0 %convolution_convert_fusion = bf16[3072,768]{1,0:T(8,128)(2,1)} fusion(bf16[768,3072]{1,0:T(8,128)(2,1)} %get-tuple-element.36, bf16[768,768]{1,0:T(8,128)(2,1)} %bitcast.19), kind=kOutput, calls=%fused_computation.17 | convolution fusion | flops 3626237952 | bytes 10616832 | tf_op jit(solution)/shard_map/rf,rd->fd/dot_general | solution.py:236
  253.9 3.0 add_add_fusion.2
  256.9 139.2 %all-reduce.3.cloned.1.call-done = f32[2392064]{0:T(1024)} async-done(((f32[2392064]{0:T(1024)}), f32[2392064]{0:T(1024)}) %all-reduce.3.cloned.1.call-update) | async-done | bytes 9568272
  396.1 1.8 fusion.111
  397.9 50.0 %reduce-scatter.3.cloned.1.call-done = bf16[192,3072]{1,0:T(8,128)(2,1)} async-done(((bf16[768,3072]{1,0:T(8,128)(2,1)}), bf16[192,3072]{1,0:T(8,128)(2,1)}) %reduce-scatter.3.cloned.1.call-update) | async-done | bytes 1179664 | tf_op jit(solution)/shard_map/reduce_scatter | solution.py:240
  447.9 8.0 %fusion.108 = (bf16[1,192,3072]{2,1,0:T(8,128)(2,1)}, f32[1,192,3072]{2,1,0:T(8,128)}, f32[1,192,3072]{2,1,0:T(8,128)}, f32[1,192,3072]{2,1,0:T(8,128)}) fusion(f32[1,192,3072]{2,1,0:T(8,128)} %param.36, bf16[192,3072]{1,0:T(8,128)(2,1)} %reduce-scatter.3.cloned.1.call-done, f32[1,192,3072]{2,1,0:T(8,128)} %param.37, f32[1,192,3072]{2,1,0:T(8,128)} %param.38), kind=kLoop, calls=%fused_computation.190 | loop fusion | flops 9437184 | bytes 16515072 | tf_op jit(solution)/shard_map/convert_element_type | solution.py:125
  455.9 45.2 %reduce-scatter.5.cloned.1.call-done = bf16[768,768]{1,0:T(8,128)(2,1)} async-done(((bf16[3072,768]{1,0:T(8,128)(2,1)}), bf16[768,768]{1,0:T(8,128)(2,1)}) %reduce-scatter.5.cloned.1.call-update) | async-done | bytes 1179664 | tf_op jit(solution)/shard_map/reduce_scatter | solution.py:243
  501.1 7.8 %fusion.105 = (bf16[1,768,768]{2,1,0:T(8,128)(2,1)}, f32[1,768,768]{2,1,0:T(8,128)}, f32[1,768,768]{2,1,0:T(8,128)}, f32[1,768,768]{2,1,0:T(8,128)}) fusion(f32[1,768,768]{2,1,0:T(8,128)} %param.39, bf16[768,768]{1,0:T(8,128)(2,1)} %reduce-scatter.5.cloned.1.call-done, f32[1,768,768]{2,1,0:T(8,128)} %param.40, f32[1,768,768]{2,1,0:T(8,128)} %param.41), kind=kLoop, calls=%fused_computation.189 | loop fusion | flops 9437184 | bytes 16515072 | tf_op jit(solution)/shard_map/convert_element_type | solution.py:125
  (174 shorter events, 20.7 us)
Async XLA Ops:
  7.2 16.4 %copy-start = (bf16[768,2304]{1,0:T(8,128)(2,1)S(1)}, bf16[768,2304]{1,0:T(8,128)(2,1)}, u32[]{:S(2)}) copy-start(bf16[768,2304]{1,0:T(8,128)(2,1)} %param.25) | copy-start | bytes 10616836
  7.2 74.5 %all-gather.3.cloned.1.call-start = ((), (), s32[]{:S(2)}) async-start(), calls=%async_computation.6 | async-start | bytes 5898240 | tf_op jit(solution)/shard_map/all_gather | solution.py:158
  20.5 5.3 %copy-start.32 = (f32[768]{0:T(1024)}, f32[768]{0:T(1024)S(1)}, u32[]{:S(2)}) copy-start(f32[768]{0:T(1024)S(1)} %get-tuple-element.21) | copy-start | bytes 9220
  20.5 19.2 %copy-start.36 = (f32[768]{0:T(1024)}, f32[768]{0:T(1024)S(1)}, u32[]{:S(2)}) copy-start(f32[768]{0:T(1024)S(1)} %get-tuple-element.20) | copy-start | bytes 9220
  21.7 4.1 copy-start.38
  23.6 3.3 copy-start.43
  25.8 6.8 %copy-start.40 = (s32[256,2]{0,1:T(2,128)S(1)}, s32[256,2]{0,1:T(2,128)}, u32[]{:S(2)}) copy-start(s32[256,2]{0,1:T(2,128)} %param.23) | copy-start | bytes 6148
  32.6 3.8 copy-start.56
  32.9 7.0 %copy-start.16 = (bf16[256,792]{0,1:T(8,128)(2,1)}, bf16[256,792]{0,1:T(8,128)(2,1)S(1)}, u32[]{:S(2)}) copy-start(bf16[256,792]{0,1:T(8,128)(2,1)S(1)} %convert_reduce_fusion) | copy-start | bytes 1216516
  33.8 2.6 copy-start.20
  33.8 2.6 copy-start.24
  35.7 1.7 copy-start.1
  35.7 1.7 copy-start.5
  35.7 2.5 copy-start.14
  36.4 2.4 copy-start.34
  37.4 2.3 copy-start.22
  38.9 0.9 copy-start.3
  38.9 4.8 copy-start.41
  40.3 0.7 copy-start.11
  41.5 1.0 copy-start.13
  43.6 30.1 %all-to-all-start = ((bf16[32,24,768]{2,1,0:T(8,128)(2,1)}), bf16[32,24,768]{2,1,0:T(8,128)(2,1)}, u32[]{:S(2)}, u32[]{:S(2)}) async-start(bf16[32,24,768]{2,1,0:T(8,128)(2,1)} %bitcast.125), calls=%async_computation | async-start | bytes 2359296 | tf_op jit(solution)/shard_map/all_to_all | solution.py:193
  51.2 68.6 %all-gather.5.cloned.1.call-start = ((), (), s32[]{:S(2)}) async-start(), calls=%async_computation.7 | async-start | bytes 5898240 | tf_op jit(solution)/shard_map/all_gather | solution.py:159
  55.3 6.4 %copy-start.47 = (f32[256]{0:T(256)}, f32[256]{0:T(256)S(1)}, u32[]{:S(2)}) copy-start(f32[256]{0:T(256)S(1)} %fusion.85) | copy-start | bytes 3076
  55.3 2.1 copy-start.58
  57.4 4.3 copy-start.27
  73.7 54.7 %all-to-all-start.2 = ((bf16[32,24,768]{2,1,0:T(8,128)(2,1)}), bf16[32,24,768]{2,1,0:T(8,128)(2,1)}, u32[]{:S(2)}, u32[]{:S(2)}) async-start(bf16[32,24,768]{2,1,0:T(8,128)(2,1)} %bitcast.126), calls=%async_computation.2 | async-start | bytes 2359296 | tf_op jit(solution)/shard_map/all_to_all | solution.py:201
  128.4 29.2 %all-to-all-start.1 = ((bf16[32,24,768]{2,1,0:T(8,128)(2,1)}), bf16[32,24,768]{2,1,0:T(8,128)(2,1)}, u32[]{:S(2)}, u32[]{:S(2)}) async-start(bf16[32,24,768]{2,1,0:T(8,128)(2,1)} %bitcast.143), calls=%async_computation.1 | async-start | bytes 2359296 | tf_op jit(solution)/shard_map/all_to_all | solution.py:195
  148.2 2.2 copy-start.59
  157.7 9.4 %copy-start.57 = (s32[256,2]{0,1:T(2,128)S(1)}, s32[256,2]{0,1:T(2,128)}, u32[]{:S(2)}) copy-start(s32[256,2]{0,1:T(2,128)} %copy-done.56) | copy-start | bytes 6148
  157.7 26.0 %all-to-all-start.3 = ((bf16[32,24,768]{2,1,0:T(8,128)(2,1)}), bf16[32,24,768]{2,1,0:T(8,128)(2,1)}, u32[]{:S(2)}, u32[]{:S(2)}) async-start(bf16[32,24,768]{2,1,0:T(8,128)(2,1)} %bitcast.142), calls=%async_computation.3 | async-start | bytes 2359296 | tf_op jit(solution)/shard_map/all_to_all | solution.py:208
  165.3 230.8 %all-reduce.3.cloned.1.call-start = ((), (), s32[]{:S(2)}) async-start(), calls=%async_computation.10 | async-start | bytes 19136512
  165.6 4.9 copy-start.48
  165.6 5.0 copy-start.12
  167.0 4.6 copy-start.31
  170.4 14.8 %copy-start.37 = (f32[768]{0:T(1024)S(1)}, f32[768]{0:T(1024)}, u32[]{:S(2)}) copy-start(f32[768]{0:T(1024)} %copy-done.36) | copy-start | bytes 9220
  172.8 15.4 %copy-start.55 = (f32[256]{0:T(256)S(1)}, f32[256]{0:T(256)}, u32[]{:S(2)}) copy-start(f32[256]{0:T(256)} %copy-done.54) | copy-start | bytes 3076
  172.8 15.4 %copy-start.42 = (f32[256]{0:T(256)S(1)}, f32[256]{0:T(256)}, u32[]{:S(2)}) copy-start(f32[256]{0:T(256)} %copy-done.41) | copy-start | bytes 3076
  172.8 15.4 %copy-start.51 = (f32[256]{0:T(256)S(1)}, f32[256]{0:T(256)}, u32[]{:S(2)}) copy-start(f32[256]{0:T(256)} %copy-done.50) | copy-start | bytes 3076
  183.7 4.6 copy-start.4
  183.7 4.6 copy-start.28
  185.2 4.2 copy-start.10
  185.2 4.2 copy-start.15
  188.3 2.4 copy-start.23
  189.3 1.3 copy-start.8
  189.3 1.3 copy-start.45
  189.4 5.2 %copy-start.35 = (f32[12,256]{1,0:T(8,128)S(1)}, f32[12,256]{1,0:T(8,128)}, u32[]{:S(2)}) copy-start(f32[12,256]{1,0:T(8,128)} %copy-done.34) | copy-start | bytes 36868
  194.6 3.0 copy-start.2
  194.6 3.0 copy-start.21
  194.6 3.0 copy-start.25
  194.6 3.2 copy-start.26
  198.8 1.0 copy-start.18
  198.8 1.6 copy-start.17
  199.8 1.0 copy-start.6
  199.8 1.0 copy-start.33
  199.8 1.0 copy-start.39
  200.8 2.6 copy-start.44
  213.5 13.6 %copy-start.52 = (f32[256]{0:T(256)}, f32[256]{0:T(256)S(1)}, u32[]{:S(2)}) copy-start(f32[256]{0:T(256)S(1)} %multiply_multiply_fusion.13) | copy-start | bytes 3076
  221.4 5.6 %copy-start.7 = (bf16[256,768]{1,0:T(8,128)(2,1)S(1)}, bf16[256,768]{1,0:T(8,128)(2,1)}, u32[]{:S(2)}) copy-start(bf16[256,768]{1,0:T(8,128)(2,1)} %param.21) | copy-start | bytes 1179652
  221.4 5.6 %copy-start.19 = (f32[256,768]{1,0:T(8,128)S(1)}, f32[256,768]{1,0:T(8,128)}, u32[]{:S(2)}) copy-start(f32[256,768]{1,0:T(8,128)} %get-tuple-element.51) | copy-start | bytes 2359300
  221.4 6.7 %copy-start.9 = (f32[589824]{0:T(1024)S(1)}, f32[589824]{0:T(1024)}, u32[]{:S(2)}) copy-start(f32[589824]{0:T(1024)} %reshape.369) | copy-start | bytes 7077892
  227.0 2.6 copy-start.29
  227.0 5.4 %copy-start.49 = (f32[768]{0:T(1024)S(1)}, f32[768]{0:T(1024)}, u32[]{:S(2)}) copy-start(f32[768]{0:T(1024)} %get-tuple-element.14) | copy-start | bytes 9220
  235.1 212.8 %reduce-scatter.3.cloned.1.call-start = ((), (), s32[]{:S(2)}) async-start(), calls=%async_computation.8 | async-start | bytes 5898240 | tf_op jit(solution)/shard_map/reduce_scatter | solution.py:240
  244.2 256.9 %reduce-scatter.5.cloned.1.call-start = ((), (), s32[]{:S(2)}) async-start(), calls=%async_computation.9 | async-start | bytes 5898240 | tf_op jit(solution)/shard_map/reduce_scatter | solution.py:243
  (5 other events, 3.2 us)
Sparse Core Ops, SparseCore 0:
  9.7 55.3 all-gather.2
  66.7 53.0 all-gather.4
  235.3 160.8 all-reduce.2
  398.4 49.5 reduce-scatter.2
  450.2 50.8 reduce-scatter.4
where the time goes:
time: 524 us; the launch traced here: 516 us
  waiting for transfers between devices  258 us (49%)
  matrix products  120 us (23%)
  local copies, waits for them, and re-layouts  52 us (10%)
  other arithmetic  39.7 us (8%)
  starting transfers between devices  31.4 us (6%)
  between operations  14.9 us (3%)
    unnamed x6, waiting for transfers between devices  140 us
    reduce_scatter x1, waiting for transfers between devices, body(): lax.psum_scatter(grad_in_full.astype(jnp.bfloat16), 'dp', scatter_dimensi...  50 us
    reduce_scatter x1, waiting for transfers between devices, body(): lax.psum_scatter(grad_out_full.astype(jnp.bfloat16), 'dp', scatter_dimens...  45.2 us
    dot_general x2, matrix products, expert_forward(): pre_act = jnp.dot(row_block, weight_in, preferred_element_type=jnp.float32)  29.9 us
    unnamed x128, local copies, waits for them, and re-layouts  20.8 us
    convert_element_type x3, other arithmetic, adamw(): return (master_new, first_new, second_new, master_new.astype(jnp.bfloat16))  17.6 us
    dot_general x2, matrix products, expert_backward(): jnp.einsum('rf,df->rd', grad_pre, weight_in, preferred_element_type=jnp.f...  14.4 us
    dot_general x2, matrix products, expert_forward(): jnp.dot(hidden, weight_out, preferred_element_type=jnp.float32)  12.8 us
  transfers between devices with their start and end apart: 9, of which 5 were waited for; matrix products, arithmetic and copies ran while one was open for 28% of the time, Pallas kernels for 0%

commit v1 on v0

--- a/solution.py
+++ b/solution.py
@@ -1,6 +1,7 @@
 import jax
 import jax.numpy as jnp
 from jax import lax
+from jax.sharding import Mesh
 from jax.sharding import PartitionSpec as P
 
 HEAD_DIM = 64
@@ -123,6 +124,88 @@
         first_hat / (jnp.sqrt(second_hat) + adam_eps) + decay_rate * master
     )
     return (master_new, first_new, second_new, master_new.astype(jnp.bfloat16))
+
+
+PLANE = ("zl", "x", "y")
+DEPTH = ("zh", "zl")
+ALL = ("zh", "zl", "x", "y", "c")
+
+
+def swap_core(block):
+    return lax.ppermute(block, "c", [(0, 1), (1, 0)])
+
+
+def along_depth(block, step):
+    return lax.ppermute(block, DEPTH, [(z, (z + step) % 4) for z in range(4)])
+
+
+def swap_pair(block):
+    return lax.ppermute(block, DEPTH, [(z, 3 - z) for z in range(4)])
+
+
+def swap_low(block):
+    return lax.ppermute(block, "zl", [(0, 1), (1, 0)])
+
+
+def gather_weight(own_half, mate_half, kind, core, zh, zl):
+    by_kind = lambda wanted: jnp.where(wanted == core, own_half, mate_half)
+    own = by_kind(kind)
+    from_below = along_depth(by_kind(1 - zh), 1)
+    from_above = along_depth(by_kind(zh), -1)
+    far_side = jnp.where(zl == 0, from_above, from_below)
+    near_side = jnp.where(zl == 0, from_below, from_above)
+    across = swap_pair(far_side)
+    z = 2 * zh + zl
+    rows = own.shape[0]
+    full = jnp.zeros((4 * rows, own.shape[1]), own.dtype)
+    for block, place in ((own, z), (far_side, z ^ 1), (near_side, 3 - z), (across, (3 - z) ^ 1)):
+        full = lax.dynamic_update_slice(full, block, (place * rows, 0))
+    return full
+
+
+def reduce_weight(partial, core, kind, zh, zl):
+    rows = partial.shape[0] // 4
+    away = lax.dynamic_slice(partial, ((1 - zh) * 2 * rows, 0), (2 * rows, partial.shape[1]))
+    kept = lax.dynamic_slice(partial, (zh * 2 * rows, 0), (2 * rows, partial.shape[1]))
+    kept = kept + swap_pair(away.astype(jnp.bfloat16)).astype(jnp.float32)
+    mine = lax.dynamic_slice(kept, (zl * rows, 0), (rows, kept.shape[1]))
+    other = lax.dynamic_slice(kept, ((1 - zl) * rows, 0), (rows, kept.shape[1]))
+    other = swap_low(other.astype(jnp.bfloat16)).astype(jnp.float32)
+    stays = jnp.where(kind == core, mine, other)
+    leaves = jnp.where(kind == core, other, mine)
+    arrived = swap_core(leaves.astype(jnp.bfloat16)).astype(jnp.float32)
+    first = jnp.where(core == 0, stays, arrived)
+    second = jnp.where(core == 0, arrived, stays)
+    return first, second
+
+
+def scatter_axis(blocks, axis):
+    here = lax.axis_index(axis)
+    total = lax.dynamic_index_in_dim(blocks, here, 0, keepdims=False)
+    for step in (1, 3, 2):
+        there = lax.rem(here + step, 4)
+        leaving = lax.dynamic_index_in_dim(blocks, there, 0, keepdims=False).astype(jnp.bfloat16)
+        moves = [(i, (i + step) % 4) for i in range(4)]
+        total = total + lax.ppermute(leaving, axis, moves).astype(jnp.float32)
+    return total
+
+
+def scatter_dense(flat, core):
+    rows = flat.shape[0] // (128 * 128)
+    blocks = flat.reshape(64, 2, rows, 128)
+    kept = lax.dynamic_index_in_dim(blocks, core, 1, keepdims=False)
+    away = lax.dynamic_index_in_dim(blocks, 1 - core, 1, keepdims=False)
+    kept = kept + swap_core(away.astype(jnp.bfloat16)).astype(jnp.float32)
+    kept = kept.reshape(4, 4, 4, rows, 128)
+    cut = 80
+    one = kept[:, :, :, :cut]
+    two = kept[:, :, :, cut:]
+    one = scatter_axis(jnp.moveaxis(one, 1, 0), "x")
+    two = scatter_axis(jnp.moveaxis(two, 2, 0), "y")
+    one = scatter_axis(jnp.moveaxis(one, 1, 0), "y")
+    two = scatter_axis(jnp.moveaxis(two, 1, 0), "x")
+    both = jnp.concatenate([one, two], axis=1)
+    return scatter_axis(both, DEPTH).reshape(-1)
 
 
 def body(
@@ -150,16 +233,21 @@
 ):
     token_count, model_width = tokens.shape
     hidden_width = frozen_in.shape[1]
+    block_width = hidden_width // 8
     expert_total = w_router.shape[1]
     capacity = 3 * token_count // expert_total + 1
-    source_count = lax.axis_size("expert")
-    group_count = lax.axis_size("dp")
-    full_in, full_out = (
-        lax.all_gather(new_in, "dp", axis=1, tiled=True),
-        lax.all_gather(new_out, "dp", axis=1, tiled=True),
-    )
-    full_in = full_in[0]
-    full_out = full_out[0]
+    core, zh, zl = (lax.axis_index(a) for a in ("c", "zh", "zl"))
+    kind = zh ^ zl
+
+    in_blocks = new_in[0].reshape(-1, 4, 2, block_width)
+    in_halves = [in_blocks[:, :, h].reshape(-1, 4 * block_width) for h in range(2)]
+    out_halves = [new_out[0][h * block_width : (h + 1) * block_width] for h in range(2)]
+    pick = lambda halves, which: jnp.where(which == 0, halves[0], halves[1])
+    in_mate = swap_core(pick(in_halves, 1 - core))
+    out_mate = swap_core(pick(out_halves, 1 - core))
+    half_in = gather_weight(pick(in_halves, core), in_mate, kind, core, zh, zl)
+    half_out = gather_weight(pick(out_halves, core), out_mate, kind, core, zh, zl)
+
     inputs = tokens.astype(jnp.float32)
     attn_in = layer_norm(inputs, norm_gains[0]).astype(jnp.bfloat16)
     qkv_low = jnp.dot(attn_in, w_qkv, preferred_element_type=jnp.float32).astype(jnp.bfloat16)
@@ -174,7 +262,11 @@
     flat_routes = routes.reshape(-1)
     onehot = (flat_routes[:, None] == expert_ids[None, :]).astype(jnp.int32)
     before = jnp.cumsum(onehot, axis=0) - onehot
-    places = flat_routes * capacity + jnp.sum(before * onehot, axis=1)
+    new_ids = flat_routes - 1
+    ordered = jnp.where(
+        flat_routes == 0, 0, 1 + 16 * ((new_ids & 1) ^ zh) + jnp.right_shift(new_ids, 1)
+    )
+    places = ordered * capacity + jnp.sum(before * onehot, axis=1)
     select_rows = (
         places[:, None] == jnp.arange(expert_total * capacity, dtype=jnp.int32)[None, :]
     ).astype(jnp.bfloat16)
@@ -183,35 +275,52 @@
         "lkp,ld->pd", select_rows, feedforward_input, preferred_element_type=jnp.float32
     ).astype(jnp.bfloat16)
     state_buffers = state_buffers.reshape(expert_total, capacity, model_width)
-    frozen_pre, frozen_result = expert_forward(state_buffers[0], frozen_in, frozen_out)
     upstream = cotangent.astype(jnp.float32)
     grad_pairs = (gate_values[:, :, None] * upstream[:, None, :]).astype(jnp.bfloat16)
     grad_results = jnp.einsum(
         "lkp,lkd->pd", select_rows, grad_pairs, preferred_element_type=jnp.float32
     ).astype(jnp.bfloat16)
     grad_results = grad_results.reshape(expert_total, capacity, model_width)
-    received = lax.all_to_all(state_buffers[1:], "expert", split_axis=0, concat_axis=0, tiled=True)
-    pre_act, result = expert_forward(received.reshape(-1, model_width), full_in, full_out)
-    sent_back = lax.all_to_all(
-        result.reshape(received.shape), "expert", split_axis=0, concat_axis=0, tiled=True
-    )
-    sent_back, pre_act = (sent_back, pre_act)
-    new_pre = pre_act.reshape(received.shape[0], received.shape[1], -1)
-    new_pre = new_pre.reshape(-1, hidden_width)
-    grad_received = lax.all_to_all(
-        grad_results[1:], "expert", split_axis=0, concat_axis=0, tiled=True
-    )
-    grad_out_rows = grad_received.reshape(-1, model_width)
-    new_hidden, new_grad_pre, new_grad_rows = expert_backward(
-        new_pre, grad_out_rows, full_in, full_out
-    )
-    grad_back = lax.all_to_all(
-        new_grad_rows.reshape(source_count, capacity, model_width),
-        "expert",
-        split_axis=0,
-        concat_axis=0,
-        tiled=True,
-    )
+
+    exchange = lambda v: lax.all_to_all(v, PLANE, split_axis=0, concat_axis=0, tiled=True)
+    received = exchange(state_buffers[1:]).reshape(-1, model_width)
+    grad_received = exchange(grad_results[1:]).reshape(-1, model_width)
+    row_count = received.shape[0]
+    rows = jnp.concatenate([received, swap_core(received)], axis=0)
+    grad_rows_in = jnp.concatenate([grad_received, swap_core(grad_received)], axis=0)
+
+    def merge(partial):
+        mate = swap_core(partial[row_count:].astype(jnp.bfloat16)).astype(jnp.float32)
+        whole = (partial[:row_count] + mate).astype(jnp.bfloat16)
+        return exchange(whole.reshape(-1, capacity, model_width))
+
+    pre_act = jnp.dot(rows, half_in, preferred_element_type=jnp.float32)
+    new_hidden, gelu_pull = jax.vjp(exact_gelu, pre_act)
+    new_hidden = new_hidden.astype(jnp.bfloat16)
+    grad_hidden = jnp.einsum("rd,fd->rf", grad_rows_in, half_out, preferred_element_type=jnp.float32)
+    new_grad_pre = gelu_pull(grad_hidden)[0].astype(jnp.bfloat16)
+    grad_out_half = jnp.einsum(
+        "rf,rd->fd", new_hidden, grad_rows_in, preferred_element_type=jnp.float32
+    )
+    out_first_half, out_second_half = reduce_weight(grad_out_half, core, kind, zh, zl)
+    grad_back = merge(
+        jnp.einsum("rf,df->rd", new_grad_pre, half_in, preferred_element_type=jnp.float32)
+    )
+    sent_back = merge(jnp.dot(new_hidden, half_out, preferred_element_type=jnp.float32))
+    grad_in_half = jnp.einsum("rd,rf->df", rows, new_grad_pre, preferred_element_type=jnp.float32)
+    in_first_half, in_second_half = reduce_weight(grad_in_half, core, kind, zh, zl)
+    grad_out_shard = jnp.concatenate([out_first_half, out_second_half], axis=0)
+    grad_in_shard = jnp.stack(
+        [
+            in_first_half.reshape(-1, 4, block_width),
+            in_second_half.reshape(-1, 4, block_width),
+        ],
+        axis=2,
+    ).reshape(-1, hidden_width)
+
+    frozen_pre, frozen_result = expert_forward(state_buffers[0], frozen_in, frozen_out)
+    frozen_parts = expert_backward(frozen_pre, grad_results[0], frozen_in, frozen_out)
+
     results = jnp.concatenate([frozen_result[None], sent_back], axis=0).reshape(
         expert_total * capacity, model_width
     )
@@ -228,22 +337,6 @@
         "ld,le->de", feedforward_input, grad_logits, preferred_element_type=jnp.float32
     )
     grad_ffn = jnp.einsum("le,de->ld", grad_logits, w_router, preferred_element_type=jnp.float32)
-    frozen_parts = expert_backward(frozen_pre, grad_results[0], frozen_in, frozen_out)
-    in_rows = received.reshape(-1, model_width)
-    grad_in_full = jnp.einsum(
-        "rd,rf->df", in_rows, new_grad_pre, preferred_element_type=jnp.float32
-    )
-    grad_out_full = jnp.einsum(
-        "rf,rd->fd", new_hidden, grad_out_rows, preferred_element_type=jnp.float32
-    )
-    grad_in_shard, grad_out_shard = (
-        lax.psum_scatter(
-            grad_in_full.astype(jnp.bfloat16), "dp", scatter_dimension=0, tiled=True
-        ).astype(jnp.float32),
-        lax.psum_scatter(
-            grad_out_full.astype(jnp.bfloat16), "dp", scatter_dimension=0, tiled=True
-        ).astype(jnp.float32),
-    )
     grad_buffers = jnp.concatenate([frozen_parts[2][None], grad_back], axis=0).reshape(
         -1, model_width
     )
@@ -266,7 +359,6 @@
     grad_attn_norm = jnp.einsum("le,de->ld", grad_qkv, w_qkv, preferred_element_type=jnp.float32)
     grad_input_norm, gain_attn_grad = norm_back(inputs, norm_gains[0], grad_attn_norm)
     input_grad = grad_middle + grad_input_norm
-    device_total = group_count * source_count
     flat_grad = jnp.concatenate(
         [
             qkv_grad.reshape(-1),
@@ -277,75 +369,24 @@
         ]
     )
     flat_grad = jnp.concatenate(
-        [
-            flat_grad,
-            jnp.zeros((dense_master.shape[0] * device_total - flat_grad.shape[0],), jnp.float32),
-        ]
-    )
-    dense_grad = lax.psum_scatter(flat_grad, ("dp", "expert"), scatter_dimension=0, tiled=True)
+        [flat_grad, jnp.zeros((dense_master.shape[0] * 128 - flat_grad.shape[0],), jnp.float32)]
+    )
+    dense_grad = scatter_dense(flat_grad, core)
     dense_new = adamw(dense_master, dense_first, dense_second, dense_grad)
     in_new = adamw(master_in, first_in, second_in, grad_in_shard[None])
     out_new = adamw(master_out, first_out, second_out, grad_out_shard[None])
-    return (
-        activations.astype(jnp.bfloat16),
-        input_grad,
-        dense_new[0],
-        dense_new[1],
-        dense_new[2],
-        dense_new[3],
-        in_new[0],
-        in_new[1],
-        in_new[2],
-        in_new[3],
-        out_new[0],
-        out_new[1],
-        out_new[2],
-        out_new[3],
-    )
+    return (activations.astype(jnp.bfloat16), input_grad) + dense_new + in_new + out_new
 
 
 def solution(mesh):
+    fine = Mesh(mesh.devices.reshape(2, 2, 4, 4, 2), ALL)
+    tokens = P(ALL, None)
+    flat = P(ALL)
+    expert = P(("x", "y", "c"), DEPTH, None)
     return jax.shard_map(
         body,
-        mesh=mesh,
-        in_specs=(
-            P(("dp", "expert"), None),
-            P(("dp", "expert"), None),
-            P(("dp", "expert"), None),
-            P(("dp", "expert"), None),
-            P(),
-            P(),
-            P(),
-            P(),
-            P(),
-            P(),
-            P("expert", "dp", None),
-            P("expert", "dp", None),
-            P(("dp", "expert")),
-            P(("dp", "expert")),
-            P(("dp", "expert")),
-            P("expert", "dp", None),
-            P("expert", "dp", None),
-            P("expert", "dp", None),
-            P("expert", "dp", None),
-            P("expert", "dp", None),
-            P("expert", "dp", None),
-        ),
-        out_specs=(
-            P(("dp", "expert"), None),
-            P(("dp", "expert"), None),
-            P(("dp", "expert")),
-            P(("dp", "expert")),
-            P(("dp", "expert")),
-            P(("dp", "expert")),
-            P("expert", "dp", None),
-            P("expert", "dp", None),
-            P("expert", "dp", None),
-            P("expert", "dp", None),
-            P("expert", "dp", None),
-            P("expert", "dp", None),
-            P("expert", "dp", None),
-            P("expert", "dp", None),
-        ),
+        mesh=fine,
+        in_specs=(tokens,) * 4 + (P(),) * 6 + (expert,) * 2 + (flat,) * 3 + (expert,) * 6,
+        out_specs=(tokens,) * 2 + (flat,) * 4 + (expert,) * 8,
         check_vma=False,
     )

time: 524 us -> 468 us (0.89)
  waiting for transfers between devices: 258 us -> 95.7 us
  local copies, waits for them, and re-layouts: 52 us -> 113 us
  other arithmetic: 39.7 us -> 81.1 us
  starting transfers between devices: 31.4 us -> 65 us
  matrix products: 120 us -> 104 us
  between operations: 14.9 us -> 2.42 us
    unnamed x6 -> x0, waiting for transfers between devices: 140 us -> none
    reduce_scatter x2 -> x0, waiting for transfers between devices: 95.2 us -> none  [the longest x1 50 us: body(): lax.psum_scatter(grad_in_full.astype(jnp.bfloat16), 'dp', scatter_dimensi...]
    ppermute x0 -> x34, waiting for transfers between devices: none -> 80.5 us  [the longest x4 23.7 us: swap_pair(): return lax.ppermute(block, DEPTH, [(z, 3 - z) for z in range(4)])]
    ppermute x0 -> x34, starting transfers between devices: none -> 34.4 us  [the longest x15 19.7 us: scatter_axis(): total = total + lax.ppermute(leaving, axis, moves).astype(jnp.float32)]
    dot_general x3 -> x6, matrix products: 30.1 us -> 58.6 us  [the longest x1 26.6 us: body(): pre_act = jnp.dot(rows, half_in, preferred_element_type=jnp.float32)]
    dot_general x2 -> x1, matrix products: 29.9 us -> 3.78 us  [expert_forward(): pre_act = jnp.dot(row_block, weight_in, preferred_element_type=jnp.float32)]
    another operation x2 -> x12, local copies, waits for them, and re-layouts: 0.02 us -> 19.2 us  [the longest x3 8.41 us: body(): jnp.stack([in_first_half.reshape(-1, 4, block_width), in_second_half.resh...]
    select_n x0 -> x6, other arithmetic: none -> 13.6 us  [the longest x3 7.16 us: gather_weight(): by_kind = lambda wanted: jnp.where(wanted == core, own_half, mate_half)]
  transfers between devices with their start and end apart: 9 -> 38, of which waited for: 5 -> 17; matrix products, arithmetic and copies ran while one was open for 28% -> 61% of each run, Pallas kernels for 0% -> 0%
where the time goes in v1:
time: 468 us; the launch traced here: 461 us
  local copies, waits for them, and re-layouts  113 us (24%)
  matrix products  104 us (22%)
  waiting for transfers between devices  95.7 us (20%)
  other arithmetic  81.1 us (17%)
  starting transfers between devices  65 us (14%)
    all_to_all x4, starting transfers between devices, body(): lax.all_to_all(v, PLANE, split_axis=0, concat_axis=0, tiled=True)  30.7 us
    unnamed x205, local copies, waits for them, and re-layouts  28.8 us
    dot_general x1, matrix products, body(): pre_act = jnp.dot(rows, half_in, preferred_element_type=jnp.float32)  26.6 us
    ppermute x4, waiting for transfers between devices, swap_pair(): return lax.ppermute(block, DEPTH, [(z, 3 - z) for z in range(4)])  23.7 us
    ppermute x4, waiting for transfers between devices, along_depth(): return lax.ppermute(block, DEPTH, [(z, (z + step) % 4) for z in range(4)])  20.4 us
    ppermute x2, waiting for transfers between devices, swap_low(): return lax.ppermute(block, 'zl', [(0, 1), (1, 0)])  19.9 us
    ppermute x15, starting transfers between devices, scatter_axis(): total = total + lax.ppermute(leaving, axis, moves).astype(jnp.float32)  19.7 us
    ppermute x15, waiting for transfers between devices, scatter_axis(): total = total + lax.ppermute(leaving, axis, moves).astype(jnp.float32)  16.5 us
  transfers between devices with their start and end apart: 38, of which 17 were waited for; matrix products, arithmetic and copies ran while one was open for 61% of the time, Pallas kernels for 0%

profile of v1, /device:TPU:0, one launch (start us, length us, event | category | flops | bytes accessed | tf_op | source)
XLA Modules:
  0.0 460.7 jit_solution(12161147992479869716)
XLA Ops:
  0.7 2.3 select_bitcast_fusion
  2.9 4.0 reshape_squeeze.2
  6.9 3.8 fusion.141
  23.9 3.2 reduce-window.6
  35.6 2.1 convolution_convert_fusion
  60.0 8.9 %all-to-all-start.2 = ((bf16[32,24,768]{2,1,0:T(8,128)(2,1)}), bf16[32,24,768]{2,1,0:T(8,128)(2,1)}, u32[]{:S(2)}, u32[]{:S(2)}) async-start(bf16[32,24,768]{2,1,0:T(8,128)(2,1)} %bitcast.199), calls=%async_computation.2 | async-start | bytes 2359296 | tf_op jit(solution)/shard_map/all_to_all | solution.py:285
  73.2 3.8 fusion.100
  77.0 7.2 %fusion.31 = bf16[1,24,768]{2,1,0:T(8,128)(2,1)} fusion(bf16[768,3072]{1,0:T(8,128)(2,1)} %param.29, f32[24,3072]{1,0:T(8,128)} %fusion.100, bf16[3072,768]{1,0:T(8,128)(2,1)} %param.30, bf16[792,768]{1,0:T(8,128)(2,1)} %copy-done.54), kind=kOutput, calls=%fused_computation.101 | convolution fusion | flops 231819264 | bytes 9805824 | tf_op jit(solution)/shard_map/rf,df->rd/dot_general | solution.py:112
  84.2 2.4 slice.108
  88.5 2.5 bitcast_select_fusion
  92.7 8.5 %all-to-all-start = ((bf16[32,24,768]{2,1,0:T(8,128)(2,1)}), bf16[32,24,768]{2,1,0:T(8,128)(2,1)}, u32[]{:S(2)}, u32[]{:S(2)}) async-start(bf16[32,24,768]{2,1,0:T(8,128)(2,1)} %bitcast.200), calls=%async_computation | async-start | bytes 2359296 | tf_op jit(solution)/shard_map/all_to_all | solution.py:285
  102.3 2.2 bitcast_select_fusion.1
  104.5 2.4 collective-permute-start.6
  107.1 2.4 broadcast_select_fusion.2
  110.2 2.5 collective-permute-start.2
  112.7 4.2 fusion.30
  116.9 2.6 all-to-all-done
  119.5 10.9 %collective-permute-done.6 = bf16[384,768]{1,0:T(8,128)(2,1)} collective-permute-done((bf16[384,768]{1,0:T(8,128)(2,1)}, bf16[384,768]{1,0:T(8,128)(2,1)}, u32[]{:S(2)}, u32[]{:S(2)}) %collective-permute-start.6) | collective-permute-done | bytes 589856 | tf_op jit(solution)/shard_map/ppermute | solution.py:139
  132.6 9.5 %collective-permute-done.2 = bf16[192,1536]{1,0:T(8,128)(2,1)} collective-permute-done((bf16[192,1536]{1,0:T(8,128)(2,1)}, bf16[192,1536]{1,0:T(8,128)(2,1)}, u32[]{:S(2)}, u32[]{:S(2)}) %collective-permute-start.2) | collective-permute-done | bytes 589856 | tf_op jit(solution)/shard_map/ppermute | solution.py:139
  147.7 11.9 %collective-permute-done.4 = bf16[192,1536]{1,0:T(8,128)(2,1)S(1)} collective-permute-done((bf16[192,1536]{1,0:T(8,128)(2,1)S(1)}, bf16[192,1536]{1,0:T(8,128)(2,1)S(1)}, u32[]{:S(2)}, u32[]{:S(2)}) %collective-permute-start.4) | collective-permute-done | bytes 589856 | tf_op jit(solution)/shard_map/ppermute | solution.py:143
  159.7 26.6 %multiply_convert_fusion = (bf16[1536,1536]{1,0:T(8,128)(2,1)S(1)}, f32[1536,1536]{1,0:T(8,128)}, f32[1536,1536]{1,0:T(8,128)}) fusion(bf16[768,1536]{1,0:T(8,128)(2,1)S(1)} %constant_dynamic-update-slice_fusion.2, bf16[768,768]{1,0:T(8,128)(2,1)S(1)} %collective-permute-done, bf16[768,768]{1,0:T(8,128)(2,1)} %bitcast.10), kind=kOutput, calls=%fused_computation.3 | convolution fusion | flops 3781951488 | bytes 28311552 | tf_op jit(solution)/shard_map/dot_general | solution.py:297
  186.3 3.8 fusion.145
  190.6 5.5 %fusion.17 = f32[1536,768]{1,0:T(8,128)S(1)} fusion(bf16[1536,1536]{1,0:T(8,128)(2,1)S(1)} %get-tuple-element.40, bf16[768,768]{1,0:T(8,128)(2,1)} %collective-permute-done.10, bf16[768,768]{1,0:T(8,128)(2,1)} %bitcast.19), kind=kOutput, calls=%fused_computation.61 | convolution fusion | flops 3628597248 | bytes 11796480 | tf_op jit(solution)/shard_map/rf,rd->fd/dot_general | solution.py:302
  200.0 12.1 %add_convert_fusion = bf16[1536,1536]{1,0:T(8,128)(2,1)} fusion(f32[1536,1536]{1,0:T(8,128)} %get-tuple-element.41, bf16[1536,768]{1,0:T(8,128)(2,1)S(1)} %constant_dynamic-update-slice_fusion, f32[1536,1536]{1,0:T(8,128)} %get-tuple-element.80, bf16[768,768]{1,0:T(8,128)(2,1)} %collective-permute-done.10, bf16[768,768]{1,0:T(8,128)(2,1)} %bitcast.19), kind=kOutput, calls=%fused_computation.2 | convolution fusion | flops 3661627392 | bytes 28311552 | tf_op jit(solution)/shard_map/rd,fd->rf/dot_general | solution.py:300
  212.1 6.7 %fusion.18 = f32[768,1536]{1,0:T(8,128)S(1)} fusion(bf16[1536,1536]{1,0:T(8,128)(2,1)} %add_convert_fusion, bf16[768,768]{1,0:T(8,128)(2,1)} %copy-done.94, bf16[768,768]{1,0:T(8,128)(2,1)} %bitcast.10), kind=kOutput, calls=%fused_computation.62 | convolution fusion | flops 3628597248 | bytes 11796480 | tf_op jit(solution)/shard_map/rd,rf->df/dot_general | solution.py:310
  218.8 2.2 copy-done.31
  222.1 3.0 collective-permute-start.28
  225.1 3.9 fusion.146
  230.3 3.2 fusion.11
  233.5 6.8 %all-to-all-start.1 = ((bf16[32,24,768]{2,1,0:T(8,128)(2,1)}), bf16[32,24,768]{2,1,0:T(8,128)(2,1)}, u32[]{:S(2)}, u32[]{:S(2)}) async-start(bf16[32,24,768]{2,1,0:T(8,128)(2,1)} %bitcast.201), calls=%async_computation.1 | async-start | bytes 2359296 | tf_op jit(solution)/shard_map/all_to_all | solution.py:285
  240.3 2.3 convert_add_fusion
  244.5 10.1 %collective-permute-done.28 = bf16[384,1536]{1,0:T(8,128)(2,1)} collective-permute-done((bf16[384,1536]{1,0:T(8,128)(2,1)}, bf16[384,1536]{1,0:T(8,128)(2,1)}, u32[]{:S(2)}, u32[]{:S(2)}) %collective-permute-start.28) | collective-permute-done | bytes 1179680 | tf_op jit(solution)/shard_map/ppermute | solution.py:143
  254.6 2.3 convert_add_fusion.1
  257.1 3.3 fusion.10
  260.4 8.7 %collective-permute-done.32 = bf16[384,768]{1,0:T(8,128)(2,1)S(1)} collective-permute-done((bf16[384,768]{1,0:T(8,128)(2,1)S(1)}, bf16[384,768]{1,0:T(8,128)(2,1)S(1)}, u32[]{:S(2)}, u32[]{:S(2)}) %collective-permute-start.32) | collective-permute-done | bytes 589856 | tf_op jit(solution)/shard_map/ppermute | solution.py:147
  270.1 11.2 %collective-permute-done.29 = bf16[192,1536]{1,0:T(8,128)(2,1)S(1)} collective-permute-done((bf16[192,1536]{1,0:T(8,128)(2,1)S(1)}, bf16[192,1536]{1,0:T(8,128)(2,1)S(1)}, u32[]{:S(2)}, u32[]{:S(2)}) %collective-permute-start.29) | collective-permute-done | bytes 589856 | tf_op jit(solution)/shard_map/ppermute | solution.py:147
  282.3 6.5 %all-to-all-start.3 = ((bf16[32,24,768]{2,1,0:T(8,128)(2,1)}), bf16[32,24,768]{2,1,0:T(8,128)(2,1)}, u32[]{:S(2)}, u32[]{:S(2)}) async-start(bf16[32,24,768]{2,1,0:T(8,128)(2,1)} %bitcast.202), calls=%async_computation.3 | async-start | bytes 2359296 | tf_op jit(solution)/shard_map/all_to_all | solution.py:285
  290.4 2.1 multiply_reduce_fusion.1
  295.0 12.7 %all-to-all-done.3 = bf16[32,24,768]{2,1,0:T(8,128)(2,1)} async-done(((bf16[32,24,768]{2,1,0:T(8,128)(2,1)}), bf16[32,24,768]{2,1,0:T(8,128)(2,1)}, u32[]{:S(2)}, u32[]{:S(2)}) %all-to-all-start.3) | async-done | bytes 1179680 | tf_op jit(solution)/shard_map/all_to_all | solution.py:285
  317.7 2.9 convolution_convert_fusion.2
  324.4 2.6 fusion.39
  327.0 4.1 fusion.49
  333.0 3.2 reshape.536
  336.9 7.9 %reshape.535 = f32[1769472]{0:T(1024)} reshape(f32[768,2304]{1,0:T(8,128)} %fusion.49) | data formatting | bytes 14155776 | tf_op jit(solution)/shard_map/reshape | solution.py:364
  344.8 5.6 %constant_dynamic-update-slice_fusion.8 = f32[2392064]{0:T(1024)} fusion(f32[1769472]{0:T(1024)} %reshape.535), kind=kLoop, calls=%fused_computation.265 | loop fusion | bytes 14155776
  358.5 10.0 %reshape.538 = f32[64,2,146,128]{3,2,1,0:T(8,128)} reshape(f32[2392064]{0:T(1024)} %broadcast_dynamic-update-slice_fusion) | data formatting | bytes 19136512 | tf_op jit(solution)/shard_map/reshape | solution.py:195
  368.5 2.8 fusion.6
  373.4 5.1 %constant_dynamic-slice_fusion.6 = f32[64,1,146,128]{3,2,1,0:T(8,128)} fusion(f32[64,2,146,128]{3,2,1,0:T(8,128)} %reshape.538, s32[]{:T(128)S(6)} %select_n.305), kind=kLoop, calls=%fused_computation.252 | loop fusion | bytes 9568260 | tf_op jit(solution)/shard_map/jit(dynamic_index_in_dim)/dynamic_slice | solution.py:196
  380.6 2.8 convert_select_fusion.5
  383.4 2.6 stack_reshape.6
  386.0 2.6 stack_reshape.7
  388.6 2.2 pad_maximum_fusion.2
  390.8 3.2 copy.363
  394.0 4.1 broadcast_in_dim_reshape.4
  398.1 8.6 %fusion.135 = (bf16[1,192,3072]{2,1,0:T(8,128)(2,1)}, f32[1,192,3072]{2,1,0:T(8,128)}, f32[1,192,3072]{2,1,0:T(8,128)}, f32[1,192,3072]{2,1,0:T(8,128)}) fusion(f32[1,192,3072]{2,1,0:T(8,128)} %param.36, f32[1,192,3072]{2,1,0:T(8,128)} %broadcast_in_dim_reshape.4, f32[1,192,3072]{2,1,0:T(8,128)} %param.37, f32[1,192,3072]{2,1,0:T(8,128)} %param.38), kind=kLoop, calls=%fused_computation.302 | loop fusion | flops 8847360 | bytes 17694720 | tf_op jit(solution)/shard_map/convert_element_type | solution.py:126
  406.7 4.3 bitcast_add_fusion
  413.5 2.4 collective-permute-start.21
  424.4 2.3 collective-permute-start.14
  430.6 2.3 collective-permute-start.23
  433.5 6.8 %collective-permute-done.13 = bf16[4,4,80,128]{3,1,0,2:T(4,128)(2,1)S(1)} collective-permute-done((bf16[4,4,80,128]{3,1,0,2:T(4,128)(2,1)S(1)}, bf16[4,4,80,128]{3,1,0,2:T(4,128)(2,1)S(1)}, u32[]{:S(2)}, u32[]{:S(2)}) %collective-permute-start.13) | collective-permute-done | bytes 327712 | tf_op jit(solution)/shard_map/ppermute | solution.py:189
  441.1 2.8 collective-permute-start.17
  446.8 3.2 collective-permute-done.18
  451.1 3.0 collective-permute-start.26
  454.8 4.7 %fusion.133 = (bf16[1,768,768]{2,1,0:T(8,128)(2,1)}, f32[1,768,768]{2,1,0:T(8,128)}, f32[1,768,768]{2,1,0:T(8,128)}, f32[1,768,768]{2,1,0:T(8,128)}) fusion(f32[1,768,768]{2,1,0:T(8,128)S(1)} %copy-done.34, f32[1,384,768]{2,1,0:T(8,128)S(1)} %get-tuple-element.45, f32[1,384,768]{2,1,0:T(8,128)S(1)} %get-tuple-element.44, f32[1,768,768]{2,1,0:T(8,128)S(1)} %copy-done.35, ...), kind=kLoop, calls=%fused_computation.301 | loop fusion | flops 9437184 | bytes 17694720 | tf_op jit(solution)/shard_map/convert_element_type | solution.py:126
  (367 shorter events, 126.2 us)
Async XLA Ops:
  0.6 35.0 %copy-start = (bf16[768,2304]{1,0:T(8,128)(2,1)S(1)}, bf16[768,2304]{1,0:T(8,128)(2,1)}, u32[]{:S(2)}) copy-start(bf16[768,2304]{1,0:T(8,128)(2,1)} %param.25) | copy-start | bytes 10616836
  2.9 85.5 %collective-permute-start.5 = (bf16[384,768]{1,0:T(8,128)(2,1)}, bf16[384,768]{1,0:T(8,128)(2,1)}, u32[]{:S(2)}, u32[]{:S(2)}) collective-permute-start(bf16[384,768]{1,0:T(8,128)(2,1)} %select_bitcast_fusion), channel_id=1, source_target_pairs={{0,1},{1,0},{2,3},{3,2},{4,5},{5,4},{6,7},{7,6},{8,9},{9,8},{10,11... | collective-permute-start | bytes 1769480 | tf_op jit(solution)/shard_map/ppermute | solution.py:135
  13.0 93.9 %collective-permute-start.1 = (bf16[192,1536]{1,0:T(8,128)(2,1)}, bf16[192,1536]{1,0:T(8,128)(2,1)}, u32[]{:S(2)}, u32[]{:S(2)}) collective-permute-start(bf16[192,1536]{1,0:T(8,128)(2,1)} %bitcast.72), channel_id=1, source_target_pairs={{0,1},{1,0},{2,3},{3,2},{4,5},{5,4},{6,7},{7,6},{8,9},{9,8},{10,11... | collective-permute-start | bytes 1769480 | tf_op jit(solution)/shard_map/ppermute | solution.py:135
  18.6 19.2 %copy-start.69 = (f32[256]{0:T(256)}, f32[256]{0:T(256)S(1)}, u32[]{:S(2)}) copy-start(f32[256]{0:T(256)S(1)} %broadcast_multiply_fusion.1) | copy-start | bytes 3076
  20.4 17.4 %copy-start.77 = (f32[256]{0:T(256)}, f32[256]{0:T(256)S(1)}, u32[]{:S(2)}) copy-start(f32[256]{0:T(256)S(1)} %fusion.110) | copy-start | bytes 3076
  21.8 16.0 %copy-start.61 = (f32[768]{0:T(1024)}, f32[768]{0:T(1024)S(1)}, u32[]{:S(2)}) copy-start(f32[768]{0:T(1024)S(1)} %get-tuple-element.21) | copy-start | bytes 9220
  60.0 32.7 %all-to-all-start.2 = ((bf16[32,24,768]{2,1,0:T(8,128)(2,1)}), bf16[32,24,768]{2,1,0:T(8,128)(2,1)}, u32[]{:S(2)}, u32[]{:S(2)}) async-start(bf16[32,24,768]{2,1,0:T(8,128)(2,1)} %bitcast.199), calls=%async_computation.2 | async-start | bytes 2359296 | tf_op jit(solution)/shard_map/all_to_all | solution.py:285
  91.0 28.5 %collective-permute-start.7 = (bf16[384,768]{1,0:T(8,128)(2,1)}, bf16[384,768]{1,0:T(8,128)(2,1)}, u32[]{:S(2)}, u32[]{:S(2)}) collective-permute-start(bf16[384,768]{1,0:T(8,128)(2,1)} %get-tuple-element.38), channel_id=1, source_target_pairs={{0,32},{32,64},{64,96},{96,0},{1,33},{33,65},{65,97},{97,1},{2,34}... | collective-permute-start | bytes 1769480 | tf_op jit(solution)/shard_map/ppermute | solution.py:139
  92.7 26.7 %all-to-all-start = ((bf16[32,24,768]{2,1,0:T(8,128)(2,1)}), bf16[32,24,768]{2,1,0:T(8,128)(2,1)}, u32[]{:S(2)}, u32[]{:S(2)}) async-start(bf16[32,24,768]{2,1,0:T(8,128)(2,1)} %bitcast.200), calls=%async_computation | async-start | bytes 2359296 | tf_op jit(solution)/shard_map/all_to_all | solution.py:285
  104.5 25.9 %collective-permute-start.6 = (bf16[384,768]{1,0:T(8,128)(2,1)}, bf16[384,768]{1,0:T(8,128)(2,1)}, u32[]{:S(2)}, u32[]{:S(2)}) collective-permute-start(bf16[384,768]{1,0:T(8,128)(2,1)} %get-tuple-element.56), channel_id=1, source_target_pairs={{0,96},{32,0},{64,32},{96,64},{1,97},{33,1},{65,33},{97,65},{2,98}... | collective-permute-start | bytes 1769480 | tf_op jit(solution)/shard_map/ppermute | solution.py:139
  106.9 5.8 %copy-start.58 = (f32[24,3072]{1,0:T(8,128)S(1)}, f32[24,3072]{1,0:T(8,128)}, u32[]{:S(2)}) copy-start(f32[24,3072]{1,0:T(8,128)} %fusion.100) | copy-start | bytes 884740
  109.5 7.4 %copy-start.38 = (bf16[768,1536]{1,0:T(8,128)(2,1)}, bf16[768,1536]{1,0:T(8,128)(2,1)S(1)}, u32[]{:S(2)}) copy-start(bf16[768,1536]{1,0:T(8,128)(2,1)S(1)} %get-tuple-element.60) | copy-start | bytes 7077892
  109.5 23.1 %collective-permute-start.3 = (bf16[192,1536]{1,0:T(8,128)(2,1)}, bf16[192,1536]{1,0:T(8,128)(2,1)}, u32[]{:S(2)}, u32[]{:S(2)}) collective-permute-start(bf16[192,1536]{1,0:T(8,128)(2,1)} %get-tuple-element.58), channel_id=1, source_target_pairs={{0,32},{32,64},{64,96},{96,0},{1,33},{33,65},{65,97},{97,1},{2,34}... | collective-permute-start | bytes 1769480 | tf_op jit(solution)/shard_map/ppermute | solution.py:139
  110.2 31.8 %collective-permute-start.2 = (bf16[192,1536]{1,0:T(8,128)(2,1)}, bf16[192,1536]{1,0:T(8,128)(2,1)}, u32[]{:S(2)}, u32[]{:S(2)}) collective-permute-start(bf16[192,1536]{1,0:T(8,128)(2,1)} %get-tuple-element.59), channel_id=1, source_target_pairs={{0,96},{32,0},{64,32},{96,64},{1,97},{33,1},{65,33},{97,65},{2,98}... | collective-permute-start | bytes 1769480 | tf_op jit(solution)/shard_map/ppermute | solution.py:139
  116.9 73.7 %collective-permute-start.10 = (bf16[768,768]{1,0:T(8,128)(2,1)}, bf16[768,768]{1,0:T(8,128)(2,1)}, u32[]{:S(2)}, u32[]{:S(2)}) collective-permute-start(bf16[768,768]{1,0:T(8,128)(2,1)} %bitcast.19), channel_id=1, source_target_pairs={{0,1},{1,0},{2,3},{3,2},{4,5},{5,4},{6,7},{7,6},{8,9},{9,8},{10,11... | collective-permute-start | bytes 3538952 | tf_op jit(solution)/shard_map/ppermute | solution.py:135
  119.5 22.6 %copy-start.39 = (bf16[768,1536]{1,0:T(8,128)(2,1)S(1)}, bf16[768,1536]{1,0:T(8,128)(2,1)}, u32[]{:S(2)}) copy-start(bf16[768,1536]{1,0:T(8,128)(2,1)} %copy-done.38) | copy-start | bytes 7077892
  119.5 40.2 %collective-permute-start = (bf16[768,768]{1,0:T(8,128)(2,1)}, bf16[768,768]{1,0:T(8,128)(2,1)S(1)}, u32[]{:S(2)}, u32[]{:S(2)}) collective-permute-start(bf16[768,768]{1,0:T(8,128)(2,1)} %bitcast.10), channel_id=1, source_target_pairs={{0,1},{1,0},{2,3},{3,2},{4,5},{5,4},{6,7},{7,6},{8,9},{9,8},{10,11... | collective-permute-start | bytes 3538952 | tf_op jit(solution)/shard_map/ppermute | solution.py:135
  132.4 11.2 %copy-start.41 = (bf16[1536,768]{1,0:T(8,128)(2,1)S(1)}, bf16[1536,768]{1,0:T(8,128)(2,1)}, u32[]{:S(2)}) copy-start(bf16[1536,768]{1,0:T(8,128)(2,1)} %get-tuple-element.36) | copy-start | bytes 7077892
  132.4 15.3 %collective-permute-start.8 = (bf16[384,768]{1,0:T(8,128)(2,1)S(1)}, bf16[384,768]{1,0:T(8,128)(2,1)S(1)}, u32[]{:S(2)}, u32[]{:S(2)}) collective-permute-start(bf16[384,768]{1,0:T(8,128)(2,1)S(1)} %get-tuple-element.37), channel_id=1, source_target_pairs={{0,96},{32,64},{64,32},{96,0},{1,97},{33,65},{65,33},{97,1},{2,98}... | collective-permute-start | bytes 1769480 | tf_op jit(solution)/shard_map/ppermute | solution.py:143
  143.3 16.4 %collective-permute-start.4 = (bf16[192,1536]{1,0:T(8,128)(2,1)S(1)}, bf16[192,1536]{1,0:T(8,128)(2,1)S(1)}, u32[]{:S(2)}, u32[]{:S(2)}) collective-permute-start(bf16[192,1536]{1,0:T(8,128)(2,1)S(1)} %get-tuple-element.43), channel_id=1, source_target_pairs={{0,96},{32,64},{64,32},{96,0},{1,97},{33,65},{65,33},{97,1},{2,98}... | collective-permute-start | bytes 1769480 | tf_op jit(solution)/shard_map/ppermute | solution.py:143
  159.7 26.6 %copy-start.94 = (bf16[768,768]{1,0:T(8,128)(2,1)}, bf16[768,768]{1,0:T(8,128)(2,1)S(1)}, u32[]{:S(2)}) copy-start(bf16[768,768]{1,0:T(8,128)(2,1)S(1)} %collective-permute-done) | copy-start | bytes 3538948
  190.3 40.0 %collective-permute-start.9 = (bf16[768,768]{1,0:T(8,128)(2,1)S(1)}, bf16[768,768]{1,0:T(8,128)(2,1)}, u32[]{:S(2)}, u32[]{:S(2)}) collective-permute-start(bf16[768,768]{1,0:T(8,128)(2,1)S(1)} %slice.143), channel_id=1, source_target_pairs={{0,1},{1,0},{2,3},{3,2},{4,5},{5,4},{6,7},{7,6},{8,9},{9,8},{10,11... | collective-permute-start | bytes 3538952 | tf_op jit(solution)/shard_map/ppermute | solution.py:135
  199.4 40.9 %collective-permute-start.31 = (bf16[768,768]{1,0:T(8,128)(2,1)}, bf16[768,768]{1,0:T(8,128)(2,1)}, u32[]{:S(2)}, u32[]{:S(2)}) collective-permute-start(bf16[768,768]{1,0:T(8,128)(2,1)} %dynamic-slice_convert_fusion.1), channel_id=1, source_target_pairs={{0,96},{32,64},{64,32},{96,0},{1,97},{33,65},{65,33},{97,1},{2,98}... | collective-permute-start | bytes 3538952 | tf_op jit(solution)/shard_map/ppermute | solution.py:143
  212.1 13.0 %copy-start.95 = (bf16[1536,1536]{1,0:T(8,128)(2,1)S(1)}, bf16[1536,1536]{1,0:T(8,128)(2,1)}, u32[]{:S(2)}) copy-start(bf16[1536,1536]{1,0:T(8,128)(2,1)} %add_convert_fusion) | copy-start | bytes 14155780
  222.1 32.4 %collective-permute-start.28 = (bf16[384,1536]{1,0:T(8,128)(2,1)}, bf16[384,1536]{1,0:T(8,128)(2,1)}, u32[]{:S(2)}, u32[]{:S(2)}) collective-permute-start(bf16[384,1536]{1,0:T(8,128)(2,1)} %dynamic-slice_convert_fusion.2), channel_id=1, source_target_pairs={{0,96},{32,64},{64,32},{96,0},{1,97},{33,65},{65,33},{97,1},{2,98}... | collective-permute-start | bytes 3538952 | tf_op jit(solution)/shard_map/ppermute | solution.py:143
  230.3 26.8 %collective-permute-start.11 = (bf16[768,768]{1,0:T(8,128)(2,1)}, bf16[768,768]{1,0:T(8,128)(2,1)}, u32[]{:S(2)}, u32[]{:S(2)}) collective-permute-start(bf16[768,768]{1,0:T(8,128)(2,1)} %slice.142), channel_id=1, source_target_pairs={{0,1},{1,0},{2,3},{3,2},{4,5},{5,4},{6,7},{7,6},{8,9},{9,8},{10,11... | collective-permute-start | bytes 3538952 | tf_op jit(solution)/shard_map/ppermute | solution.py:135
  233.5 48.8 %all-to-all-start.1 = ((bf16[32,24,768]{2,1,0:T(8,128)(2,1)}), bf16[32,24,768]{2,1,0:T(8,128)(2,1)}, u32[]{:S(2)}, u32[]{:S(2)}) async-start(bf16[32,24,768]{2,1,0:T(8,128)(2,1)} %bitcast.201), calls=%async_computation.1 | async-start | bytes 2359296 | tf_op jit(solution)/shard_map/all_to_all | solution.py:285
  242.6 26.5 %copy-start.11 = (f32[768,768]{1,0:T(8,128)}, f32[768,768]{1,0:T(8,128)S(1)}, u32[]{:S(2)}) copy-start(f32[768,768]{1,0:T(8,128)S(1)} %convert_add_fusion) | copy-start | bytes 7077892
  242.7 14.4 %copy-start.33 = (f32[1536,768]{1,0:T(8,128)S(1)}, f32[1536,768]{1,0:T(8,128)}, u32[]{:S(2)}) copy-start(f32[1536,768]{1,0:T(8,128)} %copy-done.32) | copy-start | bytes 14155780
  242.7 26.4 %collective-permute-start.32 = (bf16[384,768]{1,0:T(8,128)(2,1)S(1)}, bf16[384,768]{1,0:T(8,128)(2,1)S(1)}, u32[]{:S(2)}, u32[]{:S(2)}) collective-permute-start(bf16[384,768]{1,0:T(8,128)(2,1)S(1)} %dynamic-slice_convert_fusion.3), channel_id=1, source_target_pairs={{0,32},{32,0},{1,33},{33,1},{2,34},{34,2},{3,35},{35,3},{4,36},{36... | collective-permute-start | bytes 1769480 | tf_op jit(solution)/shard_map/ppermute | solution.py:147
  256.9 24.4 %copy-start.13 = (f32[384,1536]{1,0:T(8,128)}, f32[384,1536]{1,0:T(8,128)S(1)}, u32[]{:S(2)}) copy-start(f32[384,1536]{1,0:T(8,128)S(1)} %convert_add_fusion.1) | copy-start | bytes 7077892
  257.0 24.3 %collective-permute-start.29 = (bf16[192,1536]{1,0:T(8,128)(2,1)S(1)}, bf16[192,1536]{1,0:T(8,128)(2,1)S(1)}, u32[]{:S(2)}, u32[]{:S(2)}) collective-permute-start(bf16[192,1536]{1,0:T(8,128)(2,1)S(1)} %dynamic-slice_convert_fusion.4), channel_id=1, source_target_pairs={{0,32},{32,0},{1,33},{33,1},{2,34},{34,2},{3,35},{35,3},{4,36},{36... | collective-permute-start | bytes 1769480 | tf_op jit(solution)/shard_map/ppermute | solution.py:147
  269.1 13.2 %copy-start.42 = (bf16[384,768]{1,0:T(8,128)(2,1)}, bf16[384,768]{1,0:T(8,128)(2,1)S(1)}, u32[]{:S(2)}) copy-start(bf16[384,768]{1,0:T(8,128)(2,1)S(1)} %collective-permute-done.32) | copy-start | bytes 1769476
  270.1 148.0 %collective-permute-start.33 = (bf16[384,768]{1,0:T(8,128)(2,1)}, bf16[384,768]{1,0:T(8,128)(2,1)}, u32[]{:S(2)}, u32[]{:S(2)}) collective-permute-start(bf16[384,768]{1,0:T(8,128)(2,1)} %fusion.27), channel_id=1, source_target_pairs={{0,1},{1,0},{2,3},{3,2},{4,5},{5,4},{6,7},{7,6},{8,9},{9,8},{10,11... | collective-permute-start | bytes 1769480 | tf_op jit(solution)/shard_map/ppermute | solution.py:135
  282.3 97.6 %collective-permute-start.30 = (bf16[192,1536]{1,0:T(8,128)(2,1)}, bf16[192,1536]{1,0:T(8,128)(2,1)}, u32[]{:S(2)}, u32[]{:S(2)}) collective-permute-start(bf16[192,1536]{1,0:T(8,128)(2,1)} %fusion.26), channel_id=1, source_target_pairs={{0,1},{1,0},{2,3},{3,2},{4,5},{5,4},{6,7},{7,6},{8,9},{9,8},{10,11... | collective-permute-start | bytes 1769480 | tf_op jit(solution)/shard_map/ppermute | solution.py:135
  282.3 25.3 %all-to-all-start.3 = ((bf16[32,24,768]{2,1,0:T(8,128)(2,1)}), bf16[32,24,768]{2,1,0:T(8,128)(2,1)}, u32[]{:S(2)}, u32[]{:S(2)}) async-start(bf16[32,24,768]{2,1,0:T(8,128)(2,1)} %bitcast.202), calls=%async_computation.3 | async-start | bytes 2359296 | tf_op jit(solution)/shard_map/all_to_all | solution.py:285
  344.8 5.6 %copy-start.7 = (bf16[256,768]{1,0:T(8,128)(2,1)S(1)}, bf16[256,768]{1,0:T(8,128)(2,1)}, u32[]{:S(2)}) copy-start(bf16[256,768]{1,0:T(8,128)(2,1)} %param.21) | copy-start | bytes 1179652
  344.8 5.6 %copy-start.27 = (f32[256,768]{1,0:T(8,128)S(1)}, f32[256,768]{1,0:T(8,128)}, u32[]{:S(2)}) copy-start(f32[256,768]{1,0:T(8,128)} %get-tuple-element.85) | copy-start | bytes 2359300
  344.8 6.7 %copy-start.15 = (f32[589824]{0:T(1024)S(1)}, f32[589824]{0:T(1024)}, u32[]{:S(2)}) copy-start(f32[589824]{0:T(1024)} %reshape.536) | copy-start | bytes 7077892
  373.3 5.3 %copy-start.10 = (f32[256,768]{1,0:T(8,128)S(1)}, f32[256,768]{1,0:T(8,128)}, u32[]{:S(2)}) copy-start(f32[256,768]{1,0:T(8,128)} %copy-done.9) | copy-start | bytes 2359300
  373.3 5.3 %copy-start.17 = (bf16[256,768]{1,0:T(8,128)(2,1)S(1)}, bf16[256,768]{1,0:T(8,128)(2,1)}, u32[]{:S(2)}) copy-start(bf16[256,768]{1,0:T(8,128)(2,1)} %param.24) | copy-start | bytes 1179652
  373.3 5.3 %copy-start.28 = (f32[256,768]{1,0:T(8,128)S(1)}, f32[256,768]{1,0:T(8,128)}, u32[]{:S(2)}) copy-start(f32[256,768]{1,0:T(8,128)} %get-tuple-element.85) | copy-start | bytes 2359300
  373.3 5.3 %copy-start.80 = (f32[256]{0:T(256)S(1)}, f32[256]{0:T(256)}, u32[]{:S(2)}) copy-start(f32[256]{0:T(256)} %copy-done.79) | copy-start | bytes 3076
  373.3 33.4 %collective-permute-start.12 = (bf16[64,146,128]{2,0,1:T(8,128)(2,1)}, bf16[64,146,128]{2,0,1:T(8,128)(2,1)}, u32[]{:S(2)}, u32[]{:S(2)}) collective-permute-start(bf16[64,146,128]{2,0,1:T(8,128)(2,1)} %copy.345), channel_id=1, source_target_pairs={{0,1},{1,0},{2,3},{3,2},{4,5},{5,4},{6,7},{7,6},{8,9},{9,8},{10,11... | collective-permute-start | bytes 7176200 | tf_op jit(solution)/shard_map/ppermute | solution.py:135
  411.4 6.8 %copy-start.12 = (f32[768,768]{1,0:T(8,128)S(1)}, f32[768,768]{1,0:T(8,128)}, u32[]{:S(2)}) copy-start(f32[768,768]{1,0:T(8,128)} %copy-done.11) | copy-start | bytes 7077892
  411.4 6.8 %copy-start.43 = (bf16[384,768]{1,0:T(8,128)(2,1)S(1)}, bf16[384,768]{1,0:T(8,128)(2,1)}, u32[]{:S(2)}) copy-start(bf16[384,768]{1,0:T(8,128)(2,1)} %copy-done.42) | copy-start | bytes 1769476
  413.5 10.9 %collective-permute-start.21 = (bf16[4,4,66,128]{3,1,2,0:T(4,128)(2,1)S(1)}, bf16[4,4,66,128]{3,1,2,0:T(4,128)(2,1)S(1)}, u32[]{:S(2)}, u32[]{:S(2)}) collective-permute-start(bf16[4,4,66,128]{3,1,2,0:T(4,128)(2,1)S(1)} %bitcast.228), channel_id=1, source_target_pairs={{0,4},{2,6},{4,0},{6,2},{1,5},{3,7},{5,1},{7,3},{8,12},{10,14},{12... | collective-permute-start | bytes 811016 | tf_op jit(solution)/shard_map/ppermute | solution.py:189
  415.9 11.9 %collective-permute-start.20 = (bf16[4,4,66,128]{3,1,2,0:T(4,128)(2,1)S(1)}, bf16[4,4,66,128]{3,1,2,0:T(4,128)(2,1)S(1)}, u32[]{:S(2)}, u32[]{:S(2)}) collective-permute-start(bf16[4,4,66,128]{3,1,2,0:T(4,128)(2,1)S(1)} %bitcast.227), channel_id=1, source_target_pairs={{0,6},{2,0},{4,2},{6,4},{1,7},{3,1},{5,3},{7,5},{8,14},{10,8},{12,... | collective-permute-start | bytes 811016 | tf_op jit(solution)/shard_map/ppermute | solution.py:189
  417.4 12.2 %collective-permute-start.19 = (bf16[4,4,66,128]{3,1,2,0:T(4,128)(2,1)S(1)}, bf16[4,4,66,128]{3,1,2,0:T(4,128)(2,1)S(1)}, u32[]{:S(2)}, u32[]{:S(2)}) collective-permute-start(bf16[4,4,66,128]{3,1,2,0:T(4,128)(2,1)S(1)} %bitcast.226), channel_id=1, source_target_pairs={{0,2},{2,4},{4,6},{6,0},{1,3},{3,5},{5,7},{7,1},{8,10},{10,12},{12... | collective-permute-start | bytes 811016 | tf_op jit(solution)/shard_map/ppermute | solution.py:189
  420.5 19.8 %collective-permute-start.13 = (bf16[4,4,80,128]{3,1,0,2:T(4,128)(2,1)S(1)}, bf16[4,4,80,128]{3,1,0,2:T(4,128)(2,1)S(1)}, u32[]{:S(2)}, u32[]{:S(2)}) collective-permute-start(bf16[4,4,80,128]{3,1,0,2:T(4,128)(2,1)S(1)} %get-tuple-element.48), channel_id=1, source_target_pairs={{0,8},{8,16},{16,24},{24,0},{1,9},{9,17},{17,25},{25,1},{2,10},{10... | collective-permute-start | bytes 983048 | tf_op jit(solution)/shard_map/ppermute | solution.py:189
  420.9 19.4 %collective-permute-start.15 = (bf16[4,4,80,128]{3,1,0,2:T(4,128)(2,1)S(1)}, bf16[4,4,80,128]{3,1,0,2:T(4,128)(2,1)S(1)}, u32[]{:S(2)}, u32[]{:S(2)}) collective-permute-start(bf16[4,4,80,128]{3,1,0,2:T(4,128)(2,1)S(1)} %get-tuple-element.49), channel_id=1, source_target_pairs={{0,16},{8,24},{16,0},{24,8},{1,17},{9,25},{17,1},{25,9},{2,18},{10... | collective-permute-start | bytes 983048 | tf_op jit(solution)/shard_map/ppermute | solution.py:189
  424.4 15.9 %collective-permute-start.14 = (bf16[4,4,80,128]{3,1,0,2:T(4,128)(2,1)S(1)}, bf16[4,4,80,128]{3,1,0,2:T(4,128)(2,1)S(1)}, u32[]{:S(2)}, u32[]{:S(2)}) collective-permute-start(bf16[4,4,80,128]{3,1,0,2:T(4,128)(2,1)S(1)} %get-tuple-element.50), channel_id=1, source_target_pairs={{0,24},{8,0},{16,8},{24,16},{1,25},{9,1},{17,9},{25,17},{2,26},{10... | collective-permute-start | bytes 983048 | tf_op jit(solution)/shard_map/ppermute | solution.py:189
  430.3 24.5 %copy-start.36 = (f32[1,768,768]{2,1,0:T(8,128)S(1)}, f32[1,768,768]{2,1,0:T(8,128)}, u32[]{:S(2)}) copy-start(f32[1,768,768]{2,1,0:T(8,128)} %param.41) | copy-start | bytes 7077892
  430.6 13.4 %collective-permute-start.23 = (bf16[4,66,128]{2,1,0:T(8,128)(2,1)S(1)}, bf16[4,66,128]{2,1,0:T(8,128)(2,1)S(1)}, u32[]{:S(2)}, u32[]{:S(2)}) collective-permute-start(bf16[4,66,128]{2,1,0:T(8,128)(2,1)S(1)} %copy.360), channel_id=1, source_target_pairs={{0,24},{8,0},{16,8},{24,16},{1,25},{9,1},{17,9},{25,17},{2,26},{10... | collective-permute-start | bytes 202760 | tf_op jit(solution)/shard_map/ppermute | solution.py:189
  432.9 12.1 %collective-permute-start.24 = (bf16[4,66,128]{2,1,0:T(8,128)(2,1)S(1)}, bf16[4,66,128]{2,1,0:T(8,128)(2,1)S(1)}, u32[]{:S(2)}, u32[]{:S(2)}) collective-permute-start(bf16[4,66,128]{2,1,0:T(8,128)(2,1)S(1)} %copy.362), channel_id=1, source_target_pairs={{0,16},{8,24},{16,0},{24,8},{1,17},{9,25},{17,1},{25,9},{2,18},{10... | collective-permute-start | bytes 202760 | tf_op jit(solution)/shard_map/ppermute | solution.py:189
  440.3 5.6 %collective-permute-start.22 = (bf16[4,66,128]{2,1,0:T(8,128)(2,1)S(1)}, bf16[4,66,128]{2,1,0:T(8,128)(2,1)S(1)}, u32[]{:S(2)}, u32[]{:S(2)}) collective-permute-start(bf16[4,66,128]{2,1,0:T(8,128)(2,1)S(1)} %copy.357), channel_id=1, source_target_pairs={{0,8},{8,16},{16,24},{24,0},{1,9},{9,17},{17,25},{25,1},{2,10},{10... | collective-permute-start | bytes 202760 | tf_op jit(solution)/shard_map/ppermute | solution.py:189
  440.3 14.5 %copy-start.35 = (f32[1,768,768]{2,1,0:T(8,128)S(1)}, f32[1,768,768]{2,1,0:T(8,128)}, u32[]{:S(2)}) copy-start(f32[1,768,768]{2,1,0:T(8,128)} %param.40) | copy-start | bytes 7077892
  440.6 14.1 %copy-start.34 = (f32[1,768,768]{2,1,0:T(8,128)S(1)}, f32[1,768,768]{2,1,0:T(8,128)}, u32[]{:S(2)}) copy-start(f32[1,768,768]{2,1,0:T(8,128)} %param.39) | copy-start | bytes 7077892
  441.1 5.6 %collective-permute-start.17 = (bf16[4,80,128]{2,1,0:T(8,128)(2,1)S(1)}, bf16[4,80,128]{2,1,0:T(8,128)(2,1)S(1)}, u32[]{:S(2)}, u32[]{:S(2)}) collective-permute-start(bf16[4,80,128]{2,1,0:T(8,128)(2,1)S(1)} %bitcast.234), channel_id=1, source_target_pairs={{0,6},{2,0},{4,2},{6,4},{1,7},{3,1},{5,3},{7,5},{8,14},{10,8},{12,... | collective-permute-start | bytes 245768 | tf_op jit(solution)/shard_map/ppermute | solution.py:189
  443.9 6.1 %collective-permute-start.18 = (bf16[4,80,128]{2,1,0:T(8,128)(2,1)S(1)}, bf16[4,80,128]{2,1,0:T(8,128)(2,1)S(1)}, u32[]{:S(2)}, u32[]{:S(2)}) collective-permute-start(bf16[4,80,128]{2,1,0:T(8,128)(2,1)S(1)} %bitcast.233), channel_id=1, source_target_pairs={{0,4},{2,6},{4,0},{6,2},{1,5},{3,7},{5,1},{7,3},{8,12},{10,14},{12... | collective-permute-start | bytes 245768 | tf_op jit(solution)/shard_map/ppermute | solution.py:189
  444.0 6.6 %collective-permute-start.16 = (bf16[4,80,128]{2,1,0:T(8,128)(2,1)S(1)}, bf16[4,80,128]{2,1,0:T(8,128)(2,1)S(1)}, u32[]{:S(2)}, u32[]{:S(2)}) collective-permute-start(bf16[4,80,128]{2,1,0:T(8,128)(2,1)S(1)} %bitcast.232), channel_id=1, source_target_pairs={{0,2},{2,4},{4,6},{6,0},{1,3},{3,5},{5,7},{7,1},{8,10},{10,12},{12... | collective-permute-start | bytes 245768 | tf_op jit(solution)/shard_map/ppermute | solution.py:189
  450.7 8.8 %collective-permute-start.25 = (bf16[146,128]{1,0:T(8,128)(2,1)S(1)}, bf16[146,128]{1,0:T(8,128)(2,1)S(1)}, u32[]{:S(2)}, u32[]{:S(2)}) collective-permute-start(bf16[146,128]{1,0:T(8,128)(2,1)S(1)} %get-tuple-element.73), channel_id=1, source_target_pairs={{0,32},{32,64},{64,96},{96,0},{1,33},{33,65},{65,97},{97,1},{2,34}... | collective-permute-start | bytes 112136 | tf_op jit(solution)/shard_map/ppermute | solution.py:189
  451.1 8.4 %collective-permute-start.26 = (bf16[146,128]{1,0:T(8,128)(2,1)S(1)}, bf16[146,128]{1,0:T(8,128)(2,1)S(1)}, u32[]{:S(2)}, u32[]{:S(2)}) collective-permute-start(bf16[146,128]{1,0:T(8,128)(2,1)S(1)} %get-tuple-element.74), channel_id=1, source_target_pairs={{0,96},{32,0},{64,32},{96,64},{1,97},{33,1},{65,33},{97,65},{2,98}... | collective-permute-start | bytes 112136 | tf_op jit(solution)/shard_map/ppermute | solution.py:189
  454.0 5.5 %collective-permute-start.27 = (bf16[146,128]{1,0:T(8,128)(2,1)S(1)}, bf16[146,128]{1,0:T(8,128)(2,1)S(1)}, u32[]{:S(2)}, u32[]{:S(2)}) collective-permute-start(bf16[146,128]{1,0:T(8,128)(2,1)S(1)} %get-tuple-element.75), channel_id=1, source_target_pairs={{0,64},{32,96},{64,0},{96,32},{1,65},{33,97},{65,1},{97,33},{2,66}... | collective-permute-start | bytes 112136 | tf_op jit(solution)/shard_map/ppermute | solution.py:189
  (70 other events, 154.0 us)
